TPU v7x, 256 devices: a whole 4x4x8 slice. The times are simulated.
256 devices in a mesh: section: 8 (over x, core), cache: 32 (over z, y).
Axes of the slice: x: 4, y: 4, z: 8, core: 2. Of those that a mesh axis runs over, the one named last changes fastest.
Arguments:
- hidden_in: bfloat16 [8, 8, 7168], P('section', None, 'cache'), may hold values from -6 to 6
- query_down: bfloat16 [8, 7168, 1536], P('section', 'cache'), may hold values from -0.0625 to 0.0625
- latent_down: bfloat16 [8, 7168, 576], P('section', 'cache'), may hold values from -0.0625 to 0.0625
- query_gain: float32 [8, 1536], P('section'), may hold values from 0.1 to 1.9
- latent_gain: float32 [8, 512], P('section'), may hold values from 0.25 to 4
- query_up: bfloat16 [8, 1536, 36864], P('section', None, 'cache'), may hold values from -0.15625 to 0.15625
- value_up: bfloat16 [8, 64, 512, 128], P('section', 'cache'), may hold values from -0.25 to 0.25
- output_proj: bfloat16 [8, 8192, 7168], P('section', 'cache'), may hold values from -0.5 to 0.5
- latent_cache: bfloat16 [8, 8, 8192, 576], P('section', None, 'cache'), may hold values from -70 to 70
- selected: int32 [8, 8, 32], P('section'), may hold values from 0 to 127, as said below
- lengths: int32 [8, 8], P('section'), may hold values from 2048 to 8192, as said below
Outputs:
- arrived: float32 [8, 8, 7168], P('section', None, 'cache')
Inputs may be any that keep to these rules, and one draw needn't show every extreme that they name: `selected`: each row names 32 different blocks, all below ceil(length / 64), among them the block holding position length - 1. `lengths`: the first sequence of every layer has all 8192 positions.
All inputs are finite; a program needn't handle non-finite values.
Results may differ from a plain program's by a relative error of at most 0.019.
Values may be sent and summed in bfloat16 or wider, within the bound.
A program may use at most 128 MiB of HBM per device.

v0:
```python
import jax
import jax.numpy as jnp
from jax import lax
from jax.sharding import PartitionSpec as P

LAT = 512
ROPE = 64
HV = 128
BLK = 64
KW = 576


def joined(part, axis, combine):
    gathered = jax.tree.map(lambda a: lax.all_gather(a, axis), part)

    def take(source):
        return jax.tree.map(lambda a: lax.dynamic_index_in_dim(a, source, 0, False), gathered)

    return lax.fori_loop(
        1, lax.axis_size(axis), lambda source, state: combine(state, take(source)), take(0)
    )


def passed_along(x, axis, by):
    devices = lax.axis_size(axis)
    return lax.ppermute(x, axis, [(i, (i + by) % devices) for i in range(devices)])


def rms_scale(values):
    return values * lax.rsqrt(jnp.mean(values * values, axis=-1, keepdims=True) + 1e-06)


def join_partials(first, second):
    top = jnp.maximum(first[0], second[0])
    left = jnp.exp(first[0] - top)
    right = jnp.exp(second[0] - top)
    return (
        top,
        first[1] * left + second[1] * right,
        first[2] * left[..., None] + second[2] * right[..., None],
    )


def on_device(
    hidden_in,
    query_down,
    latent_down,
    query_gain,
    latent_gain,
    query_up,
    value_up,
    output_proj,
    latent_cache,
    selected,
    lengths,
):
    hidden_row = hidden_in[0]
    seq_count = hidden_row.shape[0]
    rank = lax.axis_index("cache")
    local_heads = value_up.shape[1]
    part_query = jnp.dot(hidden_row, query_down[0], preferred_element_type=jnp.float32)
    part_kv = jnp.dot(hidden_row, latent_down[0], preferred_element_type=jnp.float32)
    query_lat, kv_new = lax.psum((part_query, part_kv), "cache")
    query_norm = (rms_scale(query_lat) * query_gain[0]).astype(jnp.bfloat16)
    new_lat = rms_scale(kv_new[:, :LAT]) * latent_gain[0]
    new_key = jnp.concatenate([new_lat, kv_new[:, LAT:]], axis=1).astype(jnp.bfloat16)
    own_queries = jnp.dot(query_norm, query_up[0], preferred_element_type=jnp.float32).astype(
        jnp.bfloat16
    )
    own_queries = own_queries.reshape(seq_count, local_heads, KW)
    all_queries = lax.all_gather(own_queries, "cache", axis=1, tiled=True)
    cache_rows = latent_cache[0]
    local_len = cache_rows.shape[1]
    start = rank * local_len
    local_blocks = start // BLK + jnp.arange(local_len // BLK, dtype=jnp.int32)
    hit = jnp.any(selected[0][:, :, None] == local_blocks[None, None, :], axis=1)
    hit = jnp.repeat(hit, BLK, axis=1)
    position = start + jnp.arange(local_len, dtype=jnp.int32)
    valid = hit & (position[None, :] < lengths[0][:, None])
    scale = (HV + ROPE) ** (-0.5)
    scores = (
        jnp.einsum("bhk,bpk->bhp", all_queries, cache_rows, preferred_element_type=jnp.float32)
        * scale
    )
    masked = jnp.where(valid[:, None, :], scores, -1e30)
    local_top = jnp.max(masked, axis=-1)
    expo = jnp.where(valid[:, None, :], jnp.exp(masked - local_top[:, :, None]), 0.0)
    local_total = jnp.sum(expo, axis=-1)
    local_sum = jnp.einsum(
        "bhp,bpc->bhc",
        expo.astype(jnp.bfloat16),
        cache_rows[:, :, :LAT],
        preferred_element_type=jnp.float32,
    )
    top_all, total_all, sum_all = joined(
        (local_top, local_total, local_sum), "cache", join_partials
    )
    head_start = rank * local_heads
    merged_top = lax.dynamic_slice_in_dim(top_all, head_start, local_heads, 1)
    merged_total = lax.dynamic_slice_in_dim(total_all, head_start, local_heads, 1)
    merged_sum = lax.dynamic_slice_in_dim(sum_all, head_start, local_heads, 1)
    new_score = (
        jnp.einsum("bhk,bk->bh", own_queries, new_key, preferred_element_type=jnp.float32) * scale
    )
    final_top = jnp.maximum(merged_top, new_score)
    carried = jnp.exp(merged_top - final_top)
    new_expo = jnp.exp(new_score - final_top)
    total = merged_total * carried + new_expo
    new_weight = new_expo.astype(jnp.bfloat16).astype(jnp.float32)
    summed = merged_sum * carried[..., None] + new_weight[..., None] * new_key[
        :, None, :LAT
    ].astype(jnp.float32)
    attended = (summed / total[..., None]).astype(jnp.bfloat16)
    head_out = jnp.einsum(
        "bhc,hcv->bhv", attended, value_up[0], preferred_element_type=jnp.float32
    ).astype(jnp.bfloat16)
    head_out = head_out.reshape(seq_count, local_heads * HV)
    partial_out = jnp.dot(head_out, output_proj[0], preferred_element_type=jnp.float32)
    projected = lax.psum_scatter(partial_out, "cache", scatter_dimension=1, tiled=True)
    layer_out = projected + hidden_row.astype(jnp.float32)
    arrived = passed_along(layer_out, "section", 1)
    return arrived[None]


def solution(mesh):
    return jax.shard_map(
        on_device,
        mesh=mesh,
        in_specs=(
            P("section", None, "cache"),
            P("section", "cache", None),
            P("section", "cache", None),
            P("section", None),
            P("section", None),
            P("section", None, "cache"),
            P("section", "cache", None, None),
            P("section", "cache", None),
            P("section", None, "cache", None),
            P("section", None, None),
            P("section", None),
        ),
        out_specs=P("section", None, "cache"),
        check_vma=False,
    )
```

profile of v0, /device:TPU:1, one launch (start us, length us, event | category | flops | bytes accessed | tf_op | source)
XLA Modules:
  0.0 788.1 jit_solution(13728052056693426692)
XLA Ops:
  6.5 1.9 fusion.25
  8.4 1.9 fusion.20
  12.4 4.3 copy.22
  17.5 133.3 %all-reduce.3.cloned.1.call-done = (f32[8,1536]{1,0:T(8,128)}, f32[8,576]{1,0:T(8,128)}) async-done(((f32[8,1536]{1,0:T(8,128)}, f32[8,576]{1,0:T(8,128)}), (f32[8,1536]{1,0:T(8,128)}, f32[8,576]{1,0:T(8,128)})) %all-reduce.3.cloned.1.call-update) | async-done | bytes 67600 | tf_op jit(solution)/shard_map/psum | solution.py:63
  151.7 2.0 fusion.8
  153.7 1.4 reshape.74
  156.0 36.6 %all_gather.21 = bf16[8,64,576]{2,0,1:T(8,128)(2,1)S(1)} all-gather(bf16[8,2,576]{2,0,1:T(8,128)(2,1)S(1)} %copy.21), channel_id=1, replica_groups=mesh['section'=8,'cache'=32] {'cache'}, dimensions={1}, use_global_device_ids=true | all-gather | bytes 608256 | tf_op jit(solution)/shard_map/all_gather | solution.py:71
  192.6 2.3 fusion.47
  195.7 1.5 fusion.11
  199.3 32.1 %all-gather.1 = f32[256,64]{1,0:T(8,128)S(1)} all-gather(f32[8,64]{1,0:T(8,128)S(1)} %fusion.24), channel_id=3, replica_groups=mesh['section'=8,'cache'=32] {'cache'}, dimensions={0}, use_global_device_ids=true | all-gather | bytes 67584 | tf_op jit(solution)/shard_map/all_gather | solution.py:14
  232.0 37.6 %all-gather = f32[256,64]{1,0:T(8,128)S(1)} all-gather(f32[8,64]{1,0:T(8,128)S(1)} %get-tuple-element.211), channel_id=2, replica_groups=mesh['section'=8,'cache'=32] {'cache'}, dimensions={0}, use_global_device_ids=true | all-gather | bytes 67584 | tf_op jit(solution)/shard_map/all_gather | solution.py:14
  273.4 171.7 %all-gather.5.cloned.1.call-done = f32[256,64,512]{2,1,0:T(8,128)} async-done(((f32[8,64,512]{2,1,0:T(8,128)}), f32[256,64,512]{2,1,0:T(8,128)}) %all-gather.5.cloned.1.call-update) | async-done | bytes 33554448 | tf_op jit(solution)/shard_map/all_gather | solution.py:14
  445.1 2.3 slice.26
  447.4 106.2 %while.19 = (s32[]{:T(128)}, f32[8,64]{1,0:T(8,128)S(1)}, f32[8,64]{1,0:T(8,128)S(1)}, f32[8,64,512]{2,1,0:T(8,128)}, f32[32,8,64]{2,1,0:T(8,128)}, /*index=5*/f...) while((s32[]{:T(128)}, f32[8,64]{1,0:T(8,128)S(1)}, ...), condition=%wide.region_6.7_spmd, body=%wide.region_5.6_spmd.sunk | while | flops 789509 | bytes 3166351 | solution.py:19
  448.0 2.7 fusion.52
  451.5 2.7 fusion.52
  454.9 2.7 fusion.52
  458.3 2.7 fusion.52
  461.7 2.7 fusion.52
  465.2 2.7 fusion.52
  468.6 2.7 fusion.52
  472.0 2.7 fusion.52
  475.4 2.7 fusion.52
  478.9 2.7 fusion.52
  482.3 2.7 fusion.52
  485.7 2.7 fusion.52
  489.1 2.7 fusion.52
  492.6 2.7 fusion.52
  496.0 2.7 fusion.52
  499.4 2.7 fusion.52
  502.9 2.7 fusion.52
  506.3 2.7 fusion.52
  509.7 2.7 fusion.52
  513.2 2.7 fusion.52
  516.6 2.7 fusion.52
  520.0 2.7 fusion.52
  523.4 2.7 fusion.52
  526.9 2.7 fusion.52
  530.3 2.7 fusion.52
  533.7 2.7 fusion.52
  537.1 2.7 fusion.52
  540.6 2.7 fusion.52
  544.0 2.7 fusion.52
  547.4 2.7 fusion.52
  550.8 2.7 fusion.52
  554.7 5.5 convolution_bitcast_fusion
  560.2 212.2 %reduce-scatter.4.cloned.1.call-done = f32[224,8]{1,0:T(8,128)} async-done(((f32[7168,8]{1,0:T(8,128)}), f32[224,8]{1,0:T(8,128)}) %reduce-scatter.4.cloned.1.call-update) | async-done | bytes 7184
  773.3 6.9 collective-permute-start
  (77 shorter events, 36.7 us)
Async XLA Ops:
  6.5 145.2 %copy-start = (bf16[1,1536,1152]{2,1,0:T(8,128)(2,1)S(1)}, bf16[1,1536,1152]{2,1,0:T(8,128)(2,1)}, u32[]{:S(2)}) copy-start(bf16[1,1536,1152]{2,1,0:T(8,128)(2,1)} %param.18) | copy-start | bytes 10616836
  6.5 144.2 %all-reduce.3.cloned.1.call-start = ((), (), s32[]{:S(2)}) async-start(), calls=%async_computation.3 | async-start | bytes 139264 | tf_op jit(solution)/shard_map/psum | solution.py:63
  10.4 434.7 %all-gather.5.cloned.1.call-start = ((), (), s32[]{:S(2)}) async-start(), calls=%async_computation.1 | async-start | bytes 34603008 | tf_op jit(solution)/shard_map/all_gather | solution.py:14
  155.1 40.6 %copy-start.1 = (bf16[1,8,256,576]{3,2,1,0:T(8,128)(2,1)S(1)}, bf16[1,8,256,576]{3,2,1,0:T(8,128)(2,1)}, u32[]{:S(2)}) copy-start(bf16[1,8,256,576]{3,2,1,0:T(8,128)(2,1)} %copy.22) | copy-start | bytes 7077892
  194.9 0.8 copy-start.2
  194.9 76.2 %copy-start.6 = (f32[1,512]{1,0:T(1,128)S(1)}, f32[1,512]{1,0:T(1,128)}, u32[]{:S(2)}) copy-start(f32[1,512]{1,0:T(1,128)} %param.17) | copy-start | bytes 6148
  197.3 575.1 %reduce-scatter.4.cloned.1.call-start = ((), (), s32[]{:S(2)}) async-start(), calls=%async_computation.2 | async-start | bytes 3784704
  231.4 0.7 copy-start.3
  269.6 0.6 copy-start.4
  560.2 213.1 %copy-start.5 = (bf16[1,8,224]{2,1,0:T(8,128)(2,1)S(1)}, bf16[1,8,224]{2,1,0:T(8,128)(2,1)}, u32[]{:S(2)}) copy-start(bf16[1,8,224]{2,1,0:T(8,128)(2,1)} %param.13) | copy-start | bytes 10756
  773.3 7.7 collective-permute-start
Sparse Core Ops, SparseCore 0:
  11.0 139.7 all-reduce.2
  197.4 247.6 all-gather.4
  560.3 211.9 reduce-scatter.3
where the time goes:
time: 791 us; the launch traced here: 788 us
  waiting for transfers between devices  518 us (65%)
  other arithmetic  114 us (14%)
  blocking collectives  106 us (13%)
  matrix products  16 us (2%)
  local copies, waits for them, and re-layouts  13.5 us (2%)
  between operations  13.2 us (2%)
    unnamed x4, waiting for transfers between devices  212 us
    all_gather x1, waiting for transfers between devices, joined(): gathered = jax.tree.map(lambda a: lax.all_gather(a, axis), part)  172 us
    psum x1, waiting for transfers between devices, on_device(): query_lat, kv_new = lax.psum((part_query, part_kv), 'cache')  133 us
    add x31, other arithmetic, join_partials(): first[2] * left[..., None] + second[2] * right[..., None]  84.7 us
    all_gather x2, blocking collectives, joined(): gathered = jax.tree.map(lambda a: lax.all_gather(a, axis), part)  69.7 us
    all_gather x1, blocking collectives, on_device(): all_queries = lax.all_gather(own_queries, 'cache', axis=1, tiled=True)  36.6 us
    add x31, other arithmetic, join_partials(): first[1] * left + second[1] * right  21.5 us
  transfers between devices with their start and end apart: 4, of which 4 were waited for; matrix products, arithmetic and copies ran while one was open for 2% of the time, Pallas kernels for 0%

commit v1 on v0

v1 whole, which is shorter than its diff:
```python
import functools

import jax
import jax.numpy as jnp
from jax import lax
from jax.experimental import pallas as pl
from jax.experimental.pallas import tpu as pltpu
from jax.sharding import PartitionSpec as P

MESH = pl.DeviceIdType.MESH
F32 = jnp.float32
BF16 = jnp.bfloat16

SEQ = 8
QL = 1536
LAT = 512
ROPE = 64
HV = 128
BLK = 64
KW = 576
PADKW = 640
NZ = 8
NY = 4
NC = NZ * NY
NSEC = 8
FEAT = 224
POS = 256
QT = QL // 128
KT = LAT // 128
TILES = QT + KT + 1
SCALE = (HV + ROPE) ** (-0.5)
NEAR_FIRST = (1, 7, 2, 6, 3, 5, 4)
FAR_FIRST = (4, 3, 5, 2, 6, 1, 7, 0)


def split_three(value):
    high = value.astype(BF16).astype(F32)
    rest = value - high
    middle = rest.astype(BF16).astype(F32)
    return high, middle, rest - middle


def two_rows(value):
    high = value.astype(BF16)
    low = (value - high.astype(F32)).astype(BF16)
    return jnp.concatenate([high.astype(F32), low.astype(F32)], axis=0).astype(BF16)


def with_stats(summed, top, total):
    lane = lax.broadcasted_iota(jnp.int32, (summed.shape[0], 128), 1)
    stats = jnp.zeros((summed.shape[0], 128), F32)
    for at, piece in enumerate(split_three(top) + split_three(total)):
        stats = jnp.where(lane == at, piece, stats)
    return jnp.concatenate([summed, stats], axis=1)


def parts_of(block):
    stats = block[:, LAT:]
    lane = lax.broadcasted_iota(jnp.int32, stats.shape, 1)
    top = jnp.sum(jnp.where(lane < 3, stats, 0.0), axis=1, keepdims=True)
    total = jnp.sum(jnp.where((lane >= 3) & (lane < 6), stats, 0.0), axis=1, keepdims=True)
    return block[:, :LAT], top, total


def merged(parts):
    top = functools.reduce(jnp.maximum, [p[1] for p in parts])
    scales = [jnp.exp(p[1] - top) for p in parts]
    total = functools.reduce(jnp.add, [p[2] * a for p, a in zip(parts, scales)])
    summed = functools.reduce(jnp.add, [p[0] * a for p, a in zip(parts, scales)])
    return summed, top, total


def kernel(
    hidden,
    query_down,
    latent_down,
    query_gain,
    latent_gain,
    query_up,
    value_up,
    output_proj,
    latent_cache,
    selected,
    lengths,
    out,
    qd,
    ld,
    qu,
    vu,
    op,
    kv,
    part,
    rs_in,
    lat,
    q_all,
    q_f32,
    o_f32,
    o_out,
    y_in,
    c_out,
    z_in,
    e_out,
    e_in,
    x_out,
    x_in,
    load_sem,
    send_sem,
    x_sem,
    rs_sem,
    ag_sem,
    qz_sem,
    qy_sem,
    dy_sem,
    dz_sem,
    e_sem,
    next_sem,
):
    sec = lax.axis_index("section")
    me = lax.axis_index("cache")
    z = me // NY
    y = me % NY
    after = lax.rem(sec + 1, NSEC)
    before = lax.rem(sec + NSEC - 1, NSEC)

    def at(dz, dy):
        return lax.rem(z + dz, NZ) * NY + lax.rem(y + dy, NY)

    def load(source, target, index):
        copy = pltpu.make_async_copy(source, target, load_sem.at[index])
        copy.start()
        return copy

    def send(source, target, send_index, recv, device):
        pltpu.make_async_remote_copy(
            src_ref=source,
            dst_ref=target,
            send_sem=send_sem.at[send_index],
            recv_sem=recv,
            device_id=device,
            device_id_type=MESH,
        ).start()

    def wait_bytes(ref, sem):
        pltpu.make_async_copy(ref, ref, sem).wait()

    qd_load = load(query_down.at[0], qd, 0)
    ld_load = load(latent_down.at[0], ld, 1)

    barrier = pltpu.get_barrier_semaphore()

    @pl.loop(1, NC)
    def _(d):
        pl.semaphore_signal(
            barrier, inc=1, device_id={"cache": lax.rem(me + d, NC)}, device_id_type=MESH
        )

    for other in (after, before):
        pl.semaphore_signal(barrier, inc=1, device_id={"section": other}, device_id_type=MESH)

    qu_load = load(query_up.at[0], qu, 2)
    kv_load = load(latent_cache.at[0], kv, 3)
    vu_load = load(value_up.at[0], vu, 4)
    op_load = load(output_proj.at[0], op, 5)

    rows = hidden[0]
    qd_load.wait()
    part_q = jnp.dot(rows, qd[...], preferred_element_type=F32)
    for t in range(QT):
        part[t] = part_q[:, t * 128 : (t + 1) * 128]
    ld_load.wait()
    part_kv = jnp.dot(rows, ld[...], preferred_element_type=F32)
    for t in range(KT):
        part[QT + t] = part_kv[:, t * 128 : (t + 1) * 128]
    empty = jnp.zeros((SEQ, 128 - ROPE), F32)
    part[QT + KT] = jnp.concatenate([part_kv[:, LAT:], empty], axis=1)
    own_rows = rows.astype(F32)
    right_rows = jnp.concatenate([own_rows[:, 128:], jnp.zeros((SEQ, 32), F32)], axis=1)
    x_out[...] = jnp.concatenate([own_rows[:, :128], right_rows], axis=0).astype(BF16)

    pl.semaphore_wait(barrier, NC + 1)
    pl.semaphore_signal(next_sem, inc=1, device_id={"section": before}, device_id_type=MESH)

    is_owner = (lax.rem(me, 2) == 0) | (me == 1)
    my_tile = jnp.where(me == 1, TILES - 1, me // 2)

    @pl.loop(0, TILES)
    def _(t):
        owner = jnp.where(t == TILES - 1, 1, 2 * t)

        @pl.when(owner != me)
        def _():
            slot = lax.rem(owner - me + NC, NC) - 1
            send(part.at[t], rs_in.at[slot], 0, rs_sem, {"cache": owner})

    send(x_out, x_in, 1, x_sem, {"section": after})

    @pl.when(is_owner)
    def _():
        wait_bytes(rs_in, rs_sem)
        total = part[my_tile]
        for slot in range(NC - 1):
            total = total + rs_in[slot]
        lat[my_tile] = total

        @pl.loop(1, NC)
        def _(d):
            send(lat.at[my_tile], lat.at[my_tile], 2, ag_sem, {"cache": lax.rem(me + d, NC)})

        wait_bytes(lat.at[pl.ds(0, TILES - 1)], ag_sem)

    @pl.when(jnp.logical_not(is_owner))
    def _():
        wait_bytes(lat, ag_sem)

    squares = lat[0] * lat[0]
    for t in range(1, QT):
        squares = squares + lat[t] * lat[t]
    mean = jnp.sum(squares, axis=1, keepdims=True) * (1.0 / QL)
    q_scale = lax.rsqrt(mean + 1e-06)
    query_norm = jnp.concatenate(
        [lat[t] * q_scale * query_gain[0:1, t * 128 : (t + 1) * 128] for t in range(QT)], axis=1
    ).astype(BF16)
    qu_load.wait()
    own = jnp.dot(query_norm, qu[...], preferred_element_type=F32)
    first = own[:, :PADKW]
    second = pltpu.roll(own[:, LAT:], PADKW - ROPE, axis=1)
    own_q = jnp.concatenate([first, second], axis=0).astype(BF16)
    q_all[0] = own_q

    for dz in (4, 3, 5, 2, 6, 1, 7):
        slot = (NZ - dz) * NY
        send(q_all.at[0], q_all.at[slot], 3, qz_sem.at[NZ - dz], {"cache": at(dz, 0)})
    for dy in (2, 1, 3):
        send(q_all.at[0], q_all.at[NY - dy], 4, qy_sem, {"cache": at(0, dy)})

    squares = lat[QT] * lat[QT]
    for t in range(1, KT):
        squares = squares + lat[QT + t] * lat[QT + t]
    mean = jnp.sum(squares, axis=1, keepdims=True) * (1.0 / LAT)
    kv_scale = lax.rsqrt(mean + 1e-06)
    new_key = jnp.concatenate(
        [
            lat[QT + t] * kv_scale * latent_gain[0:1, t * 128 : (t + 1) * 128]
            for t in range(KT)
        ]
        + [lat[QT + KT]],
        axis=1,
    )
    new_key = new_key.astype(BF16).astype(F32)
    new_key = jnp.concatenate([new_key, new_key], axis=0)
    new_score = jnp.sum(own_q.astype(F32) * new_key, axis=1, keepdims=True) * SCALE

    chosen = selected[0]
    lane = lax.broadcasted_iota(jnp.int32, (SEQ, POS), 1)
    hits = jnp.zeros((SEQ, POS), F32)
    for j in range(POS // BLK):
        hit = jnp.where(chosen == me * (POS // BLK) + j, 1.0, 0.0)
        hit = jnp.max(hit, axis=1, keepdims=True)
        hits = jnp.where(lane // BLK == j, hit, hits)
    position = lax.broadcasted_iota(jnp.int32, (1, POS), 1) + me * POS

    for r in NEAR_FIRST:
        block = q_all.at[r * NY]
        wait_bytes(block, qz_sem.at[r])
        for dy in (2, 1, 3):
            send(block, q_all.at[r * NY + NY - dy], 4, qy_sem, {"cache": at(0, dy)})
    wait_bytes(q_all.at[pl.ds(0, NC - NZ)], qy_sem)

    for r in range(NZ):
        for dy in range(NY):
            block = r * NY + dy
            wide = q_all[block].astype(F32)
            for t in range(KT + 1):
                q_f32[t, block * 16 : block * 16 + 16, :] = wide[:, t * 128 : (t + 1) * 128]

    kv_load.wait()
    for b in range(SEQ):
        queries = jnp.concatenate(
            [q_f32[t, pl.ds(b, 64, stride=SEQ), :] for t in range(KT + 1)], axis=1
        )
        queries = queries[:, :KW].astype(BF16)
        keys = kv[b]
        scores = (
            jnp.dot(queries, keys, preferred_element_type=F32) * SCALE
        )
        valid = (hits[b : b + 1, :] > 0.5) & (position < lengths[0, b])
        masked = jnp.where(valid, scores, -1e30)
        top = jnp.max(masked, axis=1, keepdims=True)
        expo = jnp.where(valid, jnp.exp(masked - top), 0.0)
        total = jnp.sum(expo, axis=1, keepdims=True)
        summed = lax.dot_general(
            expo.astype(BF16),
            keys[:LAT],
            (((1,), (1,)), ((), ())),
            preferred_element_type=F32,
        )
        wide = with_stats(summed, top, total)
        for t in range(KT + 1):
            o_f32[t, pl.ds(b, 64, stride=SEQ), :] = wide[:, t * 128 : (t + 1) * 128]

    def own_block(block):
        return jnp.concatenate(
            [o_f32[t, block * 16 : block * 16 + 16, :] for t in range(KT + 1)], axis=1
        )

    for r in FAR_FIRST:
        for dy in (2, 1, 3):
            block = r * NY + dy
            o_out[block] = own_block(block).astype(BF16)
            send(o_out.at[block], y_in.at[r, NY - 1 - dy], 5, dy_sem.at[r], {"cache": at(0, dy)})
    for r in FAR_FIRST:
        wait_bytes(y_in.at[r], dy_sem.at[r])
        parts = [parts_of(own_block(r * NY))]
        parts += [parts_of(y_in[r, k].astype(F32)) for k in range(NY - 1)]
        joined = merged(parts)
        if r > 0:
            c_out[r - 1] = with_stats(*joined).astype(BF16)
            send(c_out.at[r - 1], z_in.at[NZ - 1 - r], 6, dz_sem, {"cache": at(r, 0)})
    wait_bytes(z_in, dz_sem)
    parts = [joined, (new_key[:, :LAT], new_score, jnp.ones((2 * SEQ, 1), F32))]
    parts += [parts_of(z_in[k].astype(F32)) for k in range(NZ - 1)]
    summed, _, total = merged(parts)
    attended = summed / total

    vu_load.wait()
    heads = []
    for h in range(2):
        both = two_rows(attended[h * SEQ : (h + 1) * SEQ, :])
        value = jnp.dot(both, vu[h], preferred_element_type=F32)
        heads.append(value[:SEQ] + value[SEQ:])
    head_out = two_rows(jnp.concatenate(heads, axis=1))
    op_load.wait()
    pl.semaphore_wait(next_sem, 1)
    width = NY * FEAT
    for r in FAR_FIRST:
        zt = lax.rem(z + r, NZ)
        columns = op[:, pl.ds(pl.multiple_of(zt * width, 128), width)]
        both = jnp.dot(head_out, columns, preferred_element_type=F32)
        projected = both[:SEQ] + both[SEQ:]
        for k in range(NY):
            start = k * FEAT // 128 * 128
            shift = k * FEAT - start
            stop = -(-(k * FEAT + FEAT) // 128) * 128
            piece = projected[:, start:stop]
            if shift:
                piece = pltpu.roll(piece, stop - start - shift, axis=1)
            block = jnp.concatenate([piece[:, :128], piece[:, 128:256]], axis=0)
            e_out[r * NY + k] = block.astype(BF16)
            slot = (NZ - r) % NZ * NY + y
            send(
                e_out.at[r * NY + k],
                e_in.at[slot],
                7,
                e_sem,
                {"section": after, "cache": zt * NY + k},
            )

    wait_bytes(x_in, x_sem)
    total = x_in[...].astype(F32)
    wait_bytes(e_in, e_sem)
    for slot in range(NC):
        total = total + e_in[slot].astype(F32)
    out[0, :, :128] = total[:SEQ]
    out[0, :, 128:] = total[SEQ:, : FEAT - 128]

    @pl.when(is_owner)
    def _():
        wait_bytes(part.at[pl.ds(0, TILES - 1)], send_sem.at[0])
        wait_bytes(rs_in, send_sem.at[2])

    @pl.when(jnp.logical_not(is_owner))
    def _():
        wait_bytes(part, send_sem.at[0])

    wait_bytes(x_out, send_sem.at[1])
    wait_bytes(q_all.at[pl.ds(0, NZ - 1)], send_sem.at[3])
    wait_bytes(q_all.at[pl.ds(0, NC - NZ)], send_sem.at[4])
    wait_bytes(o_out.at[pl.ds(0, NC - NZ)], send_sem.at[5])
    wait_bytes(c_out, send_sem.at[6])
    wait_bytes(e_out, send_sem.at[7])


def on_device(*arrays):
    arrays = list(arrays)
    arrays[8] = jnp.swapaxes(arrays[8], 2, 3)
    vmem = pl.BlockSpec(memory_space=pltpu.VMEM)
    smem = pl.BlockSpec(memory_space=pltpu.SMEM)
    hbm = pl.BlockSpec(memory_space=pl.ANY)
    dma = pltpu.SemaphoreType.DMA
    return pl.pallas_call(
        kernel,
        out_shape=jax.ShapeDtypeStruct((1, SEQ, FEAT), F32),
        in_specs=[vmem, hbm, hbm, vmem, vmem, hbm, hbm, hbm, hbm, vmem, smem],
        out_specs=vmem,
        scratch_shapes=[
            pltpu.VMEM((FEAT, QL), BF16),
            pltpu.VMEM((FEAT, KW), BF16),
            pltpu.VMEM((QL, 2 * KW), BF16),
            pltpu.VMEM((2, LAT, HV), BF16),
            pltpu.VMEM((2 * HV, NC * FEAT), BF16),
            pltpu.VMEM((SEQ, KW, POS), BF16),
            pltpu.VMEM((TILES, SEQ, 128), F32),
            pltpu.VMEM((NC - 1, SEQ, 128), F32),
            pltpu.VMEM((TILES, SEQ, 128), F32),
            pltpu.VMEM((NC, 16, PADKW), BF16),
            pltpu.VMEM((KT + 1, NC * 16, 128), F32),
            pltpu.VMEM((KT + 1, NC * 16, 128), F32),
            pltpu.VMEM((NC, 16, PADKW), BF16),
            pltpu.VMEM((NZ, NY - 1, 16, PADKW), BF16),
            pltpu.VMEM((NZ - 1, 16, PADKW), BF16),
            pltpu.VMEM((NZ - 1, 16, PADKW), BF16),
            pltpu.VMEM((NC, 16, 128), BF16),
            pltpu.VMEM((NC, 16, 128), BF16),
            pltpu.VMEM((16, 128), BF16),
            pltpu.VMEM((16, 128), BF16),
            dma((6,)),
            dma((8,)),
            dma,
            dma,
            dma,
            dma((NZ,)),
            dma,
            dma((NZ,)),
            dma,
            dma,
            pltpu.SemaphoreType.REGULAR,
        ],
        compiler_params=pltpu.CompilerParams(
            collective_id=0, has_side_effects=True, vmem_limit_bytes=60 << 20
        ),
        cost_estimate=pl.CostEstimate(
            flops=400_000_000, bytes_accessed=11_000_000, transcendentals=200_000
        ),
    )(*arrays)


def solution(mesh):
    return jax.shard_map(
        on_device,
        mesh=mesh,
        in_specs=(
            P("section", None, "cache"),
            P("section", "cache", None),
            P("section", "cache", None),
            P("section", None),
            P("section", None),
            P("section", None, "cache"),
            P("section", "cache", None, None),
            P("section", "cache", None),
            P("section", None, "cache", None),
            P("section", None, None),
            P("section", None),
        ),
        out_specs=P("section", None, "cache"),
        check_vma=False,
    )
```

time: 791 us -> 57.3 us (0.07)
  waiting for transfers between devices: 518 us -> 0 us
  other arithmetic: 114 us -> 0 us
  blocking collectives: 106 us -> 0 us
  Pallas kernels: 0 us -> 55.8 us
  matrix products: 16 us -> 0 us
  between operations: 13.2 us -> 0.01 us
  local copies, waits for them, and re-layouts: 13.5 us -> 1.3 us
    unnamed x4 -> x0, waiting for transfers between devices: 212 us -> none
    all_gather x1 -> x0, waiting for transfers between devices: 172 us -> none  [joined(): gathered = jax.tree.map(lambda a: lax.all_gather(a, axis), part)]
    psum x1 -> x0, waiting for transfers between devices: 133 us -> none  [on_device(): query_lat, kv_new = lax.psum((part_query, part_kv), 'cache')]
    all_gather x3 -> x0, blocking collectives: 106 us -> none  [the longest x2 69.7 us: joined(): gathered = jax.tree.map(lambda a: lax.all_gather(a, axis), part)]
    add x65 -> x0, other arithmetic: 106 us -> none  [the longest x31 84.7 us: join_partials(): first[2] * left[..., None] + second[2] * right[..., None]]
    pallas_call x0 -> x1, Pallas kernels: none -> 55.8 us  [on_device(): pl.pallas_call(kernel, out_shape=jax.ShapeDtypeStruct((1, SEQ, FEAT), F32...]
    dot_general x6 -> x0, matrix products: 10.5 us -> none  [the longest x1 2.29 us: on_device(): jnp.einsum('bhk,bpk->bhp', all_queries, cache_rows, preferred_element_typ...]
  transfers between devices with their start and end apart: 4 -> 0, of which waited for: 4 -> 0; matrix products, arithmetic and copies ran while one was open for 2% -> 0% of each run, Pallas kernels for 0% -> 0%
where the time goes in v1:
time: 57.3 us; the launch traced here: 57.1 us
  Pallas kernels  55.8 us (97%)
  local copies, waits for them, and re-layouts  1.3 us (2%)
    pallas_call x1, Pallas kernels, on_device(): pl.pallas_call(kernel, out_shape=jax.ShapeDtypeStruct((1, SEQ, FEAT), F32...  55.8 us
    unnamed x1, local copies, waits for them, and re-layouts  1.3 us

profile of v1, /device:TPU:1, one launch (start us, length us, event | category | flops | bytes accessed | tf_op | source)
XLA Modules:
  0.0 57.1 jit_solution(1040115624199211981)
XLA Ops:
  0.0 55.8 %shard_map.109 = f32[1,8,224]{2,1,0:T(8,128)} custom-call(bf16[1,8,224]{2,1,0:T(8,128)(2,1)} %hidden.1, bf16[1,224,1536]{2,1,0:T(8,128)(2,1)} %query_down.1, bf16[1,224,576]{2,1,0:T(8,128)(2,1)} %latent_down.1, f32[1,1536]{1,0:T(1,128)} %query_gain.1, f32[1,512]{1,0:T(1,128)} %latent_gain.1, bf16[1,1536,1152]{2,1,0:T(8,128)(2,1)} %query_up.1, ...), custom_call_target="tpu_custom_call" | custom-call | flops 400000000 | bytes 11000000 | tf_op jit(solution)/shard_map/pallas_call | solution.py:390
  55.8 1.3 %copy.13 = f32[1,8,224]{2,1,0:T(8,128)} copy(f32[1,8,224]{2,1,0:T(8,128)} %shard_map.109) | data formatting | bytes 14336

commit v2 on v1

v2 whole, which is shorter than its diff:
```python
import functools

import jax
import jax.numpy as jnp
from jax import lax
from jax.experimental import pallas as pl
from jax.experimental.pallas import tpu as pltpu
from jax.sharding import PartitionSpec as P

MESH = pl.DeviceIdType.MESH
F32 = jnp.float32
BF16 = jnp.bfloat16

SEQ = 8
QL = 1536
LAT = 512
ROPE = 64
HV = 128
BLK = 64
KW = 576
PADKW = 640
NZ = 8
NY = 4
NC = NZ * NY
NSEC = 8
FEAT = 224
POS = 256
QT = QL // 128
KT = LAT // 128
SCALE = (HV + ROPE) ** (-0.5)
ORDER = (0, 1, 7, 2, 6, 3, 5, 4)
GROUPS = (ORDER[:4], ORDER[4:])
GROUP_OF = {r: g for g, group in enumerate(GROUPS) for r in group}
SEND_ORDER = ((2, 7, 1, 0), (4, 5, 3, 6))
FAR_FIRST = (4, 3, 5, 2, 6, 1, 7, 0)
HALF = 4 * NY * 16


def split_three(value):
    high = value.astype(BF16).astype(F32)
    rest = value - high
    middle = rest.astype(BF16).astype(F32)
    return high, middle, rest - middle


def two_rows(value):
    high = value.astype(BF16)
    low = (value - high.astype(F32)).astype(BF16)
    return jnp.concatenate([high.astype(F32), low.astype(F32)], axis=0).astype(BF16)


def folded(value):
    half = value.shape[0] // 2
    return value[:half] + value[half:]


def stats_tile(top, total, places=0):
    lane = lax.broadcasted_iota(jnp.int32, (top.shape[0], 128), 1) - places
    stats = jnp.zeros((top.shape[0], 128), F32)
    for at, piece in enumerate(split_three(top) + split_three(total)):
        stats = jnp.where(lane == at, piece, stats)
    return stats


def read_stats(stats, place=0):
    lane = lax.broadcasted_iota(jnp.int32, stats.shape, 1) - place
    top = jnp.where((lane >= 0) & (lane < 3), stats, 0.0)
    total = jnp.where((lane >= 3) & (lane < 6), stats, 0.0)
    return jnp.sum(top, axis=1, keepdims=True), jnp.sum(total, axis=1, keepdims=True)


def merged(parts):
    top = functools.reduce(jnp.maximum, [p[1] for p in parts])
    scales = [jnp.exp(p[1] - top) for p in parts]
    total = functools.reduce(jnp.add, [p[2] * a for p, a in zip(parts, scales)])
    summed = functools.reduce(jnp.add, [p[0] * a for p, a in zip(parts, scales)])
    return summed, top, total


def kernel(
    hidden,
    query_down,
    latent_down,
    query_gain,
    latent_gain,
    query_up,
    value_up,
    output_proj,
    latent_cache,
    selected,
    lengths,
    out,
    hid,
    qgain,
    lgain,
    chosen,
    limits,
    qd,
    ld,
    qu,
    vu,
    op,
    kv,
    part_q,
    part_k,
    y_q,
    y_k,
    own_qs,
    own_ks,
    z_q,
    z_k,
    lat_q,
    lat_k,
    q_all,
    q_rope,
    q_f32,
    o_f32,
    s_f32,
    o_out,
    s_out,
    y_in,
    ys_in,
    c_out,
    z_in,
    e_out,
    e_in,
    x_out,
    x_in,
    load_sem,
    send_sem,
    recv_sem,
    qz_sem,
    qy_sem,
    rope_sem,
    dy_sem,
    ds_sem,
    next_sem,
):
    sec = lax.axis_index("section")
    me = lax.axis_index("cache")
    z = me // NY
    y = me % NY
    after = lax.rem(sec + 1, NSEC)
    before = lax.rem(sec + NSEC - 1, NSEC)

    def at(dz, dy):
        return {"cache": lax.rem(z + dz, NZ) * NY + lax.rem(y + dy, NY)}

    def load(source, target, index):
        copy = pltpu.make_async_copy(source, target, load_sem.at[index])
        copy.start()
        return copy

    def send(source, target, send_index, recv, device):
        pltpu.make_async_remote_copy(
            src_ref=source,
            dst_ref=target,
            send_sem=send_sem.at[send_index],
            recv_sem=recv,
            device_id=device,
            device_id_type=MESH,
        ).start()

    def wait_bytes(ref, sem):
        pltpu.make_async_copy(ref, ref, sem).wait()

    barrier = pltpu.get_barrier_semaphore()
    for dz in (4, 3, 5, 2, 6, 1, 7):
        pl.semaphore_signal(barrier, inc=1, device_id=at(dz, 0), device_id_type=MESH)
    for dy in (2, 1, 3):
        pl.semaphore_signal(barrier, inc=1, device_id=at(0, dy), device_id_type=MESH)
    for other in (after, before):
        pl.semaphore_signal(barrier, inc=1, device_id={"section": other}, device_id_type=MESH)

    hid_load = load(hidden.at[0], hid, 0)
    qd_load = load(query_down.at[0], qd, 1)
    ld_load = load(latent_down.at[0], ld, 2)
    qgain_load = load(query_gain, qgain, 3)
    lgain_load = load(latent_gain, lgain, 4)
    chosen_load = load(selected.at[0], chosen, 5)
    limits_load = load(lengths, limits, 6)
    qu_load = load(query_up.at[0], qu, 7)
    kv_load = load(latent_cache.at[0], kv, 8)
    vu_load = load(value_up.at[0], vu, 9)
    op_load = load(output_proj.at[0], op, 10)

    hid_load.wait()
    rows = hid[...]
    qd_load.wait()
    wide = jnp.dot(rows, qd[...], preferred_element_type=F32)
    for t in range(QT):
        part_q[t // 3, t % 3] = wide[:, t * 128 : (t + 1) * 128]

    pl.semaphore_wait(barrier, NZ + NY)

    for dy in (2, 1, 3):
        chunk = part_q.at[lax.rem(y + dy, NY)]
        send(chunk, y_q.at[NY - 1 - dy], 0, recv_sem.at[0], at(0, dy))
    ld_load.wait()
    wide = jnp.dot(rows, ld[...], preferred_element_type=F32)
    empty = jnp.zeros((SEQ, 128 - ROPE), F32)
    rope = jnp.concatenate([wide[:, LAT:], empty], axis=1)
    for t in range(KT):
        part_k[t, 0] = wide[:, t * 128 : (t + 1) * 128]
        part_k[t, 1] = rope
    for dy in (2, 1, 3):
        chunk = part_k.at[lax.rem(y + dy, NY)]
        send(chunk, y_k.at[NY - 1 - dy], 1, recv_sem.at[1], at(0, dy))
    own_rows = rows.astype(F32)
    right_rows = jnp.concatenate([own_rows[:, 128:], jnp.zeros((SEQ, 32), F32)], axis=1)
    x_out[...] = jnp.concatenate([own_rows[:, :128], right_rows], axis=0).astype(BF16)
    send(x_out, x_in, 2, recv_sem.at[2], {"section": after})

    wait_bytes(y_q, recv_sem.at[0])
    own_qs[...] = part_q[y] + y_q[0] + y_q[1] + y_q[2]
    for dz in (4, 3, 5, 2, 6, 1, 7):
        send(own_qs, z_q.at[NZ - 1 - dz], 3, recv_sem.at[3], at(dz, 0))
    wait_bytes(y_k, recv_sem.at[1])
    own_ks[...] = part_k[y] + y_k[0] + y_k[1] + y_k[2]
    for dz in (4, 3, 5, 2, 6, 1, 7):
        send(own_ks, z_k.at[NZ - 1 - dz], 4, recv_sem.at[4], at(dz, 0))

    wait_bytes(z_q, recv_sem.at[3])
    lat_q[y] = functools.reduce(jnp.add, [own_qs[...]] + [z_q[k] for k in range(NZ - 1)])
    for dy in (2, 1, 3):
        send(lat_q.at[y], lat_q.at[y], 5, recv_sem.at[5], at(0, dy))
    pl.semaphore_signal(next_sem, inc=1, device_id={"section": before}, device_id_type=MESH)
    wait_bytes(z_k, recv_sem.at[4])
    sums = functools.reduce(jnp.add, [own_ks[...]] + [z_k[k] for k in range(NZ - 1)])
    lat_k[y] = sums[0]
    new_rope = sums[1]
    for dy in (2, 1, 3):
        send(lat_k.at[y], lat_k.at[y], 6, recv_sem.at[6], at(0, dy))
    qgain_load.wait()
    qu_load.wait()
    wait_bytes(lat_q.at[pl.ds(0, NY - 1)], recv_sem.at[5])

    tiles = [lat_q[t // 3, t % 3] for t in range(QT)]
    squares = functools.reduce(jnp.add, [tile * tile for tile in tiles])
    mean = jnp.sum(squares, axis=1, keepdims=True) * (1.0 / QL)
    q_scale = lax.rsqrt(mean + 1e-06)
    query_norm = jnp.concatenate(
        [tiles[t] * q_scale * qgain[0:1, t * 128 : (t + 1) * 128] for t in range(QT)], axis=1
    ).astype(BF16)
    own = jnp.dot(query_norm, qu[...], preferred_element_type=F32)
    first = own[:, :PADKW]
    second = pltpu.roll(own[:, LAT:], PADKW - ROPE, axis=1)
    own_q = jnp.concatenate([first, second], axis=0).astype(BF16)
    q_all[0] = own_q[:, :LAT]
    q_rope[0, 0] = own_q[:, LAT:]

    for dz in (4, 3, 5, 2, 6, 1, 7):
        slot = (NZ - dz) * NY
        send(q_all.at[0], q_all.at[slot], 7, qz_sem.at[NZ - dz], at(dz, 0))
    for dy in (2, 1, 3):
        send(q_rope.at[0, 0], q_rope.at[0, NY - dy], 8, rope_sem.at[2], at(0, dy))
    for dy in (2, 1, 3):
        send(q_all.at[0], q_all.at[NY - dy], 9, qy_sem.at[0], at(0, dy))

    wait_bytes(lat_k.at[pl.ds(0, NY - 1)], recv_sem.at[6])
    lgain_load.wait()
    tiles = [lat_k[t] for t in range(KT)]
    squares = functools.reduce(jnp.add, [tile * tile for tile in tiles])
    mean = jnp.sum(squares, axis=1, keepdims=True) * (1.0 / LAT)
    kv_scale = lax.rsqrt(mean + 1e-06)
    new_key = jnp.concatenate(
        [tiles[t] * kv_scale * lgain[0:1, t * 128 : (t + 1) * 128] for t in range(KT)]
        + [new_rope],
        axis=1,
    )
    new_key = new_key.astype(BF16).astype(F32)
    new_key = jnp.concatenate([new_key, new_key], axis=0)
    new_score = jnp.sum(own_q.astype(F32) * new_key, axis=1, keepdims=True) * SCALE

    chosen_load.wait()
    picked = chosen[...]
    lane = lax.broadcasted_iota(jnp.int32, (SEQ, POS), 1)
    hits = jnp.zeros((SEQ, POS), F32)
    for j in range(POS // BLK):
        hit = jnp.where(picked == me * (POS // BLK) + j, 1.0, 0.0)
        hit = jnp.max(hit, axis=1, keepdims=True)
        hits = jnp.where(lane // BLK == j, hit, hits)
    position = lax.broadcasted_iota(jnp.int32, (1, POS), 1) + me * POS
    limits_load.wait()

    def forward(r):
        block = q_all.at[r * NY]
        wait_bytes(block, qz_sem.at[r])
        for dy in (2, 1, 3):
            target = q_all.at[r * NY + NY - dy]
            send(block, target, 9, qy_sem.at[GROUP_OF[r]], at(0, dy))

    forward(1)
    forward(7)
    wait_bytes(q_rope.at[0, pl.ds(0, NY - 1)], rope_sem.at[2])
    for dz in (4, 3, 5, 2, 6, 1, 7):
        r = NZ - dz
        send(q_rope.at[0], q_rope.at[r], 10, rope_sem.at[GROUP_OF[r]], at(dz, 0))
    for r in ORDER[3:]:
        forward(r)

    kv_load.wait()
    row = lax.broadcasted_iota(jnp.int32, (HALF // SEQ, 1), 0)
    places = row // (2 * NY) * 6

    def attend(g):
        wait_bytes(q_all.at[pl.ds(0, 4 * (NY - 1))], qy_sem.at[g])
        wait_bytes(q_rope.at[pl.ds(0, 3 + g)], rope_sem.at[g])
        base = g * HALF
        for p, r in enumerate(GROUPS[g]):
            for k in range(NY):
                rows_at = base + (p * NY + k) * 16
                block = q_all[r * NY + k].astype(F32)
                for t in range(KT):
                    q_f32[t, rows_at : rows_at + 16, :] = block[:, t * 128 : (t + 1) * 128]
                q_f32[KT, rows_at : rows_at + 16, :] = q_rope[r, k].astype(F32)
        for b in range(SEQ):
            queries = jnp.concatenate(
                [q_f32[t, pl.ds(base + b, HALF // SEQ, stride=SEQ), :] for t in range(KT + 1)],
                axis=1,
            )
            queries = queries[:, :KW].astype(BF16)
            keys = kv[b]
            scores = jnp.dot(queries, keys, preferred_element_type=F32) * SCALE
            valid = (hits[b : b + 1, :] > 0.5) & (position < limits[0, b])
            masked = jnp.where(valid, scores, -1e30)
            top = jnp.max(masked, axis=1, keepdims=True)
            expo = jnp.where(valid, jnp.exp(masked - top), 0.0)
            total = jnp.sum(expo, axis=1, keepdims=True)
            summed = folded(
                lax.dot_general(
                    two_rows(expo),
                    keys[:LAT],
                    (((1,), (1,)), ((), ())),
                    preferred_element_type=F32,
                )
            )
            rows_at = pl.ds(base + b, HALF // SEQ, stride=SEQ)
            for t in range(KT):
                o_f32[t, rows_at, :] = summed[:, t * 128 : (t + 1) * 128]
            s_f32[rows_at, :] = stats_tile(top, total, places)

    def rows_of(g, p, k):
        start = g * HALF + (p * NY + k) * 16
        return slice(start, start + 16)

    def sums_of(g, p, k):
        return jnp.concatenate([o_f32[t, rows_of(g, p, k), :] for t in range(KT)], axis=1)

    def send_sums(g):
        for k in (2, 1, 3):
            stats = [s_f32[rows_of(g, p, k), :] for p in range(4)]
            s_out[g, k] = functools.reduce(jnp.add, stats).astype(BF16)
            send(s_out.at[g, k], ys_in.at[g, NY - 1 - k], 11, ds_sem.at[g], at(0, k))
        for r in SEND_ORDER[g]:
            p = GROUPS[g].index(r)
            for k in (2, 1, 3):
                o_out[r, k] = sums_of(g, p, k).astype(BF16)
                send(o_out.at[r, k], y_in.at[r, NY - 1 - k], 12, dy_sem.at[r], at(0, k))

    def join_sums(g):
        wait_bytes(ys_in.at[g], ds_sem.at[g])
        for r in SEND_ORDER[g]:
            p = GROUPS[g].index(r)
            wait_bytes(y_in.at[r], dy_sem.at[r])
            parts = [(sums_of(g, p, 0), *read_stats(s_f32[rows_of(g, p, 0), :], 6 * p))]
            for k in range(NY - 1):
                stats = read_stats(ys_in[g, k].astype(F32), 6 * p)
                parts.append((y_in[r, k].astype(F32), *stats))
            summed, top, total = merged(parts)
            if r == 0:
                return summed, top, total
            wide = jnp.concatenate([summed, stats_tile(top, total)], axis=1)
            c_out[r - 1] = wide.astype(BF16)
            send(c_out.at[r - 1], z_in.at[NZ - 1 - r], 13, recv_sem.at[7], at(r, 0))

    attend(0)
    send_sums(0)
    attend(1)
    send_sums(1)
    own_part = join_sums(0)
    join_sums(1)
    wait_bytes(z_in, recv_sem.at[7])
    parts = [own_part, (new_key[:, :LAT], new_score, jnp.ones((2 * SEQ, 1), F32))]
    for k in range(NZ - 1):
        block = z_in[k].astype(F32)
        parts.append((block[:, :LAT], *read_stats(block[:, LAT:])))
    summed, _, total = merged(parts)
    attended = summed / total

    vu_load.wait()
    heads = []
    for h in range(2):
        both = two_rows(attended[h * SEQ : (h + 1) * SEQ, :])
        heads.append(folded(jnp.dot(both, vu[h], preferred_element_type=F32)))
    head_out = two_rows(jnp.concatenate(heads, axis=1))
    op_load.wait()
    pl.semaphore_wait(next_sem, 1)
    width = NY * FEAT
    for r in FAR_FIRST:
        zt = lax.rem(z + r, NZ)
        columns = op[:, pl.ds(pl.multiple_of(zt * width, 128), width)]
        projected = folded(jnp.dot(head_out, columns, preferred_element_type=F32))
        for k in range(NY):
            start = k * FEAT // 128 * 128
            shift = k * FEAT - start
            stop = -(-(k * FEAT + FEAT) // 128) * 128
            piece = projected[:, start:stop]
            if shift:
                piece = pltpu.roll(piece, stop - start - shift, axis=1)
            block = jnp.concatenate([piece[:, :128], piece[:, 128:256]], axis=0)
            e_out[r * NY + k] = block.astype(BF16)
            slot = (NZ - r) % NZ * NY + y
            target = {"section": after, "cache": zt * NY + k}
            send(e_out.at[r * NY + k], e_in.at[slot], 14, recv_sem.at[8], target)

    wait_bytes(x_in, recv_sem.at[2])
    total = x_in[...].astype(F32)
    wait_bytes(e_in, recv_sem.at[8])
    for slot in range(NC):
        total = total + e_in[slot].astype(F32)
    out[0, :, :128] = total[:SEQ]
    out[0, :, 128:] = total[SEQ:, : FEAT - 128]

    wait_bytes(y_q, send_sem.at[0])
    wait_bytes(y_k, send_sem.at[1])
    wait_bytes(x_out, send_sem.at[2])
    wait_bytes(z_q, send_sem.at[3])
    wait_bytes(z_k, send_sem.at[4])
    wait_bytes(lat_q.at[pl.ds(0, NY - 1)], send_sem.at[5])
    wait_bytes(lat_k.at[pl.ds(0, NY - 1)], send_sem.at[6])
    wait_bytes(q_all.at[pl.ds(0, NZ - 1)], send_sem.at[7])
    wait_bytes(q_rope.at[0, pl.ds(0, NY - 1)], send_sem.at[8])
    wait_bytes(q_all.at[pl.ds(0, NC - NZ)], send_sem.at[9])
    wait_bytes(q_rope.at[pl.ds(0, NZ - 1)], send_sem.at[10])
    wait_bytes(ys_in, send_sem.at[11])
    wait_bytes(y_in, send_sem.at[12])
    wait_bytes(z_in, send_sem.at[13])
    wait_bytes(e_out, send_sem.at[14])


def on_device(*arrays):
    arrays = list(arrays)
    arrays[8] = jnp.swapaxes(arrays[8], 2, 3)
    vmem = pl.BlockSpec(memory_space=pltpu.VMEM)
    hbm = pl.BlockSpec(memory_space=pl.ANY)
    dma = pltpu.SemaphoreType.DMA
    return pl.pallas_call(
        kernel,
        out_shape=pltpu.VMEM((1, SEQ, FEAT), F32),
        in_specs=[hbm] * 11,
        out_specs=vmem,
        scratch_shapes=[
            pltpu.VMEM((SEQ, FEAT), BF16),
            pltpu.VMEM((1, QL), F32),
            pltpu.VMEM((1, LAT), F32),
            pltpu.VMEM((SEQ, 32), jnp.int32),
            pltpu.SMEM((1, SEQ), jnp.int32),
            pltpu.VMEM((FEAT, QL), BF16),
            pltpu.VMEM((FEAT, KW), BF16),
            pltpu.VMEM((QL, 2 * KW), BF16),
            pltpu.VMEM((2, LAT, HV), BF16),
            pltpu.VMEM((2 * HV, NC * FEAT), BF16),
            pltpu.VMEM((SEQ, KW, POS), BF16),
            pltpu.VMEM((NY, 3, SEQ, 128), F32),
            pltpu.VMEM((NY, 2, SEQ, 128), F32),
            pltpu.VMEM((NY - 1, 3, SEQ, 128), F32),
            pltpu.VMEM((NY - 1, 2, SEQ, 128), F32),
            pltpu.VMEM((3, SEQ, 128), F32),
            pltpu.VMEM((2, SEQ, 128), F32),
            pltpu.VMEM((NZ - 1, 3, SEQ, 128), F32),
            pltpu.VMEM((NZ - 1, 2, SEQ, 128), F32),
            pltpu.VMEM((NY, 3, SEQ, 128), F32),
            pltpu.VMEM((NY, SEQ, 128), F32),
            pltpu.VMEM((NC, 16, LAT), BF16),
            pltpu.VMEM((NZ, NY, 16, 128), BF16),
            pltpu.VMEM((KT + 1, NC * 16, 128), F32),
            pltpu.VMEM((KT, NC * 16, 128), F32),
            pltpu.VMEM((NC * 16, 128), F32),
            pltpu.VMEM((NZ, NY, 16, LAT), BF16),
            pltpu.VMEM((2, NY, 16, 128), BF16),
            pltpu.VMEM((NZ, NY - 1, 16, LAT), BF16),
            pltpu.VMEM((2, NY - 1, 16, 128), BF16),
            pltpu.VMEM((NZ - 1, 16, PADKW), BF16),
            pltpu.VMEM((NZ - 1, 16, PADKW), BF16),
            pltpu.VMEM((NC, 16, 128), BF16),
            pltpu.VMEM((NC, 16, 128), BF16),
            pltpu.VMEM((16, 128), BF16),
            pltpu.VMEM((16, 128), BF16),
            dma((11,)),
            dma((15,)),
            dma((9,)),
            dma((NZ,)),
            dma((2,)),
            dma((3,)),
            dma((NZ,)),
            dma((2,)),
            pltpu.SemaphoreType.REGULAR,
        ],
        compiler_params=pltpu.CompilerParams(
            collective_id=0, has_side_effects=True, vmem_limit_bytes=60 << 20
        ),
        cost_estimate=pl.CostEstimate(
            flops=400_000_000, bytes_accessed=11_000_000, transcendentals=200_000
        ),
    )(*arrays)


def solution(mesh):
    return jax.shard_map(
        on_device,
        mesh=mesh,
        in_specs=(
            P("section", None, "cache"),
            P("section", "cache", None),
            P("section", "cache", None),
            P("section", None),
            P("section", None),
            P("section", None, "cache"),
            P("section", "cache", None, None),
            P("section", "cache", None),
            P("section", None, "cache", None),
            P("section", None, None),
            P("section", None),
        ),
        out_specs=P("section", None, "cache"),
        check_vma=False,
    )
```

time: 57.3 us -> 53.6 us (0.935)
  Pallas kernels: 55.8 us -> 52.9 us
  local copies, waits for them, and re-layouts: 1.3 us -> 0.6 us
    pallas_call x1, Pallas kernels: 55.8 us -> 52.9 us  [on_device(): pl.pallas_call(kernel, out_shape=pltpu.VMEM((1, SEQ, FEAT), F32), in_spec...]
    unnamed x1, local copies, waits for them, and re-layouts: 1.3 us -> 0.6 us
where the time goes in v2:
time: 53.6 us; the launch traced here: 53.5 us
  Pallas kernels  52.9 us (99%)
  local copies, waits for them, and re-layouts  0.6 us (1%)
    pallas_call x1, Pallas kernels, on_device(): pl.pallas_call(kernel, out_shape=pltpu.VMEM((1, SEQ, FEAT), F32), in_spec...  52.9 us

profile of v2, /device:TPU:1, one launch (start us, length us, event | category | flops | bytes accessed | tf_op | source)
XLA Modules:
  0.0 53.5 jit_solution(15264627129629169971)
XLA Ops:
  0.0 52.9 %shard_map.109 = f32[1,8,224]{2,1,0:T(8,128)S(1)} custom-call(bf16[1,8,224]{2,1,0:T(8,128)(2,1)} %hidden.1, bf16[1,224,1536]{2,1,0:T(8,128)(2,1)} %query_down.1, bf16[1,224,576]{2,1,0:T(8,128)(2,1)} %latent_down.1, f32[1,1536]{1,0:T(1,128)} %query_gain.1, f32[1,512]{1,0:T(1,128)} %latent_gain.1, bf16[1,1536,1152]{2,1,0:T(8,128)(2,1)} %query_up.1, ...), custom_call_target="tpu_custom_call" | custom-call | flops 400000000 | bytes 11000000 | tf_op jit(solution)/shard_map/pallas_call | solution.py:448
  52.9 0.6 %copy.13 = f32[1,8,224]{2,1,0:T(8,128)} copy(f32[1,8,224]{2,1,0:T(8,128)S(1)} %shard_map.109) | data formatting | bytes 14336

commit v3 on v2

--- a/solution.py
+++ b/solution.py
@@ -28,12 +28,13 @@
 QT = QL // 128
 KT = LAT // 128
 SCALE = (HV + ROPE) ** (-0.5)
-ORDER = (0, 1, 7, 2, 6, 3, 5, 4)
-GROUPS = (ORDER[:4], ORDER[4:])
-GROUP_OF = {r: g for g, group in enumerate(GROUPS) for r in group}
-SEND_ORDER = ((2, 7, 1, 0), (4, 5, 3, 6))
+GROUPS = ((0, 1, 7, 2, 6, 3, 5, 4),)
+DIRECT_Q = (1, 7, 2, 6)
+DIRECT_SUM = (2, 6, 1, 7)
+SUM_ORDER = ((4, 3, 5, 0),)
+ORDER = sum(GROUPS, ())
+STARTS = tuple(sum(len(group) for group in GROUPS[:g]) * NY * 16 for g in range(len(GROUPS)))
 FAR_FIRST = (4, 3, 5, 2, 6, 1, 7, 0)
-HALF = 4 * NY * 16
 
 
 def split_three(value):
@@ -113,6 +114,7 @@
     lat_k,
     q_all,
     q_rope,
+    r_in,
     q_f32,
     o_f32,
     s_f32,
@@ -122,6 +124,8 @@
     ys_in,
     c_out,
     z_in,
+    f_out,
+    f_in,
     e_out,
     e_in,
     x_out,
@@ -247,13 +251,20 @@
     second = pltpu.roll(own[:, LAT:], PADKW - ROPE, axis=1)
     own_q = jnp.concatenate([first, second], axis=0).astype(BF16)
     q_all[0] = own_q[:, :LAT]
-    q_rope[0, 0] = own_q[:, LAT:]
+    lane = lax.broadcasted_iota(jnp.int32, (SEQ, 128), 1)
+    pair = jnp.where(lane < ROPE, own[:, LAT : LAT + 128], own[:, 2 * KW - 128 :])
+    r_in[0] = jnp.concatenate([pair, jnp.zeros((SEQ, 128), F32)], axis=0).astype(BF16)
 
     for dz in (4, 3, 5, 2, 6, 1, 7):
-        slot = (NZ - dz) * NY
-        send(q_all.at[0], q_all.at[slot], 7, qz_sem.at[NZ - dz], at(dz, 0))
-    for dy in (2, 1, 3):
-        send(q_rope.at[0, 0], q_rope.at[0, NY - dy], 8, rope_sem.at[2], at(0, dy))
+        r = NZ - dz
+        if r in DIRECT_Q:
+            for dy in (2, 1, 3, 0):
+                target = q_all.at[r * NY + (NY - dy) % NY]
+                send(q_all.at[0], target, 7, qy_sem.at[r], at(dz, dy))
+        else:
+            send(q_all.at[0], q_all.at[r * NY], 7, qz_sem.at[r], at(dz, 0))
+    for dy in (2, 1, 3):
+        send(r_in.at[0], r_in.at[NY - dy], 8, rope_sem.at[0], at(0, dy))
     for dy in (2, 1, 3):
         send(q_all.at[0], q_all.at[NY - dy], 9, qy_sem.at[0], at(0, dy))
 
@@ -288,35 +299,47 @@
         wait_bytes(block, qz_sem.at[r])
         for dy in (2, 1, 3):
             target = q_all.at[r * NY + NY - dy]
-            send(block, target, 9, qy_sem.at[GROUP_OF[r]], at(0, dy))
-
-    forward(1)
-    forward(7)
-    wait_bytes(q_rope.at[0, pl.ds(0, NY - 1)], rope_sem.at[2])
+            send(block, target, 9, qy_sem.at[r], at(0, dy))
+
+    wait_bytes(r_in.at[pl.ds(0, NY - 1)], rope_sem.at[0])
+    for k in range(2):
+        two = [r_in[2 * k].astype(F32)[:SEQ], r_in[2 * k + 1].astype(F32)[:SEQ]]
+        q_rope[0, k] = jnp.concatenate(two, axis=0).astype(BF16)
     for dz in (4, 3, 5, 2, 6, 1, 7):
         r = NZ - dz
-        send(q_rope.at[0], q_rope.at[r], 10, rope_sem.at[GROUP_OF[r]], at(dz, 0))
-    for r in ORDER[3:]:
-        forward(r)
+        send(q_rope.at[0], q_rope.at[r], 10, rope_sem.at[r], at(dz, 0))
+    for r in (1, 7, 2, 6, 3, 5, 4):
+        if r not in DIRECT_Q:
+            forward(r)
 
     kv_load.wait()
-    row = lax.broadcasted_iota(jnp.int32, (HALF // SEQ, 1), 0)
-    places = row // (2 * NY) * 6
 
     def attend(g):
-        wait_bytes(q_all.at[pl.ds(0, 4 * (NY - 1))], qy_sem.at[g])
-        wait_bytes(q_rope.at[pl.ds(0, 3 + g)], rope_sem.at[g])
-        base = g * HALF
+        base = STARTS[g]
+        heads = len(GROUPS[g]) * NY * 2
+        row = lax.broadcasted_iota(jnp.int32, (heads, 1), 0)
+        places = row // (2 * NY) * 6
         for p, r in enumerate(GROUPS[g]):
+            arriving = NY if r in DIRECT_Q else NY - 1
+            wait_bytes(q_all.at[pl.ds(0, arriving)], qy_sem.at[r])
+            if r > 0:
+                wait_bytes(q_rope.at[r], rope_sem.at[r])
             for k in range(NY):
                 rows_at = base + (p * NY + k) * 16
                 block = q_all[r * NY + k].astype(F32)
                 for t in range(KT):
                     q_f32[t, rows_at : rows_at + 16, :] = block[:, t * 128 : (t + 1) * 128]
-                q_f32[KT, rows_at : rows_at + 16, :] = q_rope[r, k].astype(F32)
+            for k in range(2):
+                two = q_rope[r, k].astype(F32)
+                other = pltpu.roll(two, ROPE, axis=1)
+                for m in range(2):
+                    rows_at = base + (p * NY + 2 * k + m) * 16
+                    own_rows = slice(m * SEQ, (m + 1) * SEQ)
+                    q_f32[KT, rows_at : rows_at + SEQ, :] = two[own_rows]
+                    q_f32[KT, rows_at + SEQ : rows_at + 16, :] = other[own_rows]
         for b in range(SEQ):
             queries = jnp.concatenate(
-                [q_f32[t, pl.ds(base + b, HALF // SEQ, stride=SEQ), :] for t in range(KT + 1)],
+                [q_f32[t, pl.ds(base + b, heads, stride=SEQ), :] for t in range(KT + 1)],
                 axis=1,
             )
             queries = queries[:, :KW].astype(BF16)
@@ -335,32 +358,44 @@
                     preferred_element_type=F32,
                 )
             )
-            rows_at = pl.ds(base + b, HALF // SEQ, stride=SEQ)
+            rows_at = pl.ds(base + b, heads, stride=SEQ)
             for t in range(KT):
                 o_f32[t, rows_at, :] = summed[:, t * 128 : (t + 1) * 128]
             s_f32[rows_at, :] = stats_tile(top, total, places)
 
     def rows_of(g, p, k):
-        start = g * HALF + (p * NY + k) * 16
+        start = STARTS[g] + (p * NY + k) * 16
         return slice(start, start + 16)
 
     def sums_of(g, p, k):
         return jnp.concatenate([o_f32[t, rows_of(g, p, k), :] for t in range(KT)], axis=1)
 
     def send_sums(g):
+        staged = [GROUPS[g].index(r) for r in SUM_ORDER[g]]
         for k in (2, 1, 3):
-            stats = [s_f32[rows_of(g, p, k), :] for p in range(4)]
+            stats = [s_f32[rows_of(g, p, k), :] for p in staged]
             s_out[g, k] = functools.reduce(jnp.add, stats).astype(BF16)
             send(s_out.at[g, k], ys_in.at[g, NY - 1 - k], 11, ds_sem.at[g], at(0, k))
-        for r in SEND_ORDER[g]:
+        for r in SUM_ORDER[g]:
             p = GROUPS[g].index(r)
             for k in (2, 1, 3):
                 o_out[r, k] = sums_of(g, p, k).astype(BF16)
                 send(o_out.at[r, k], y_in.at[r, NY - 1 - k], 12, dy_sem.at[r], at(0, k))
+        for f, r in enumerate(DIRECT_SUM):
+            if r in GROUPS[g]:
+                p = GROUPS[g].index(r)
+                to = DIRECT_SUM.index(NZ - r) * NY
+                for k in (2, 1, 3, 0):
+                    stats = s_f32[rows_of(g, p, k), :]
+                    stats = pltpu.roll(stats, (128 - 6 * p) % 128, axis=1) if p else stats
+                    wide = jnp.concatenate([sums_of(g, p, k), stats], axis=1)
+                    f_out[f * NY + k] = wide.astype(BF16)
+                    target = f_in.at[to + (NY - k) % NY]
+                    send(f_out.at[f * NY + k], target, 15, recv_sem.at[9], at(r, k))
 
     def join_sums(g):
         wait_bytes(ys_in.at[g], ds_sem.at[g])
-        for r in SEND_ORDER[g]:
+        for r in SUM_ORDER[g]:
             p = GROUPS[g].index(r)
             wait_bytes(y_in.at[r], dy_sem.at[r])
             parts = [(sums_of(g, p, 0), *read_stats(s_f32[rows_of(g, p, 0), :], 6 * p))]
@@ -371,21 +406,28 @@
             if r == 0:
                 return summed, top, total
             wide = jnp.concatenate([summed, stats_tile(top, total)], axis=1)
-            c_out[r - 1] = wide.astype(BF16)
-            send(c_out.at[r - 1], z_in.at[NZ - 1 - r], 13, recv_sem.at[7], at(r, 0))
-
-    attend(0)
-    send_sums(0)
-    attend(1)
-    send_sums(1)
-    own_part = join_sums(0)
-    join_sums(1)
-    wait_bytes(z_in, recv_sem.at[7])
-    parts = [own_part, (new_key[:, :LAT], new_score, jnp.ones((2 * SEQ, 1), F32))]
-    for k in range(NZ - 1):
-        block = z_in[k].astype(F32)
-        parts.append((block[:, :LAT], *read_stats(block[:, LAT:])))
-    summed, _, total = merged(parts)
+            c_out[r] = wide.astype(BF16)
+            send(c_out.at[r], z_in.at[NZ - r], 13, recv_sem.at[7], at(r, 0))
+
+    for g in range(len(GROUPS)):
+        attend(g)
+        send_sums(g)
+    own_parts = [join_sums(g) for g in range(len(GROUPS))]
+    parts = [part for part in own_parts if part is not None]
+    parts.append((new_key[:, :LAT], new_score, jnp.ones((2 * SEQ, 1), F32)))
+
+    def joined_with(parts, blocks):
+        for block in blocks:
+            block = block.astype(F32)
+            parts = parts + [(block[:, :LAT], *read_stats(block[:, LAT:]))]
+        return merged(parts)
+
+    if DIRECT_SUM:
+        wait_bytes(f_in, recv_sem.at[9])
+        parts = [joined_with(parts, [f_in[k] for k in range(len(DIRECT_SUM) * NY)])]
+    staged = sum(SUM_ORDER, ())
+    wait_bytes(z_in.at[pl.ds(0, len(staged) - 1)], recv_sem.at[7])
+    summed, _, total = joined_with(parts, [z_in[r] for r in range(1, NZ) if r in staged])
     attended = summed / total
 
     vu_load.wait()
@@ -429,13 +471,16 @@
     wait_bytes(z_k, send_sem.at[4])
     wait_bytes(lat_q.at[pl.ds(0, NY - 1)], send_sem.at[5])
     wait_bytes(lat_k.at[pl.ds(0, NY - 1)], send_sem.at[6])
-    wait_bytes(q_all.at[pl.ds(0, NZ - 1)], send_sem.at[7])
-    wait_bytes(q_rope.at[0, pl.ds(0, NY - 1)], send_sem.at[8])
-    wait_bytes(q_all.at[pl.ds(0, NC - NZ)], send_sem.at[9])
+    straight = len(DIRECT_Q)
+    wait_bytes(q_all.at[pl.ds(0, NZ - 1 + (NY - 1) * straight)], send_sem.at[7])
+    wait_bytes(r_in.at[pl.ds(0, NY - 1)], send_sem.at[8])
+    wait_bytes(q_all.at[pl.ds(0, (NZ - straight) * (NY - 1))], send_sem.at[9])
     wait_bytes(q_rope.at[pl.ds(0, NZ - 1)], send_sem.at[10])
     wait_bytes(ys_in, send_sem.at[11])
-    wait_bytes(y_in, send_sem.at[12])
-    wait_bytes(z_in, send_sem.at[13])
+    wait_bytes(y_in.at[pl.ds(0, len(staged))], send_sem.at[12])
+    wait_bytes(z_in.at[pl.ds(0, len(staged) - 1)], send_sem.at[13])
+    if DIRECT_SUM:
+        wait_bytes(f_out, send_sem.at[15])
     wait_bytes(e_out, send_sem.at[14])
 
 
@@ -473,28 +518,31 @@
             pltpu.VMEM((NY, 3, SEQ, 128), F32),
             pltpu.VMEM((NY, SEQ, 128), F32),
             pltpu.VMEM((NC, 16, LAT), BF16),
-            pltpu.VMEM((NZ, NY, 16, 128), BF16),
+            pltpu.VMEM((NZ, 2, 16, 128), BF16),
+            pltpu.VMEM((NY, 16, 128), BF16),
             pltpu.VMEM((KT + 1, NC * 16, 128), F32),
             pltpu.VMEM((KT, NC * 16, 128), F32),
             pltpu.VMEM((NC * 16, 128), F32),
             pltpu.VMEM((NZ, NY, 16, LAT), BF16),
-            pltpu.VMEM((2, NY, 16, 128), BF16),
+            pltpu.VMEM((len(GROUPS), NY, 16, 128), BF16),
             pltpu.VMEM((NZ, NY - 1, 16, LAT), BF16),
-            pltpu.VMEM((2, NY - 1, 16, 128), BF16),
-            pltpu.VMEM((NZ - 1, 16, PADKW), BF16),
-            pltpu.VMEM((NZ - 1, 16, PADKW), BF16),
+            pltpu.VMEM((len(GROUPS), NY - 1, 16, 128), BF16),
+            pltpu.VMEM((NZ, 16, PADKW), BF16),
+            pltpu.VMEM((NZ, 16, PADKW), BF16),
+            pltpu.VMEM((max(1, len(DIRECT_SUM)) * NY, 16, PADKW), BF16),
+            pltpu.VMEM((max(1, len(DIRECT_SUM)) * NY, 16, PADKW), BF16),
             pltpu.VMEM((NC, 16, 128), BF16),
             pltpu.VMEM((NC, 16, 128), BF16),
             pltpu.VMEM((16, 128), BF16),
             pltpu.VMEM((16, 128), BF16),
             dma((11,)),
-            dma((15,)),
-            dma((9,)),
+            dma((16,)),
+            dma((10,)),
             dma((NZ,)),
-            dma((2,)),
-            dma((3,)),
             dma((NZ,)),
-            dma((2,)),
+            dma((NZ,)),
+            dma((NZ,)),
+            dma((len(GROUPS),)),
             pltpu.SemaphoreType.REGULAR,
         ],
         compiler_params=pltpu.CompilerParams(

time: 53.6 us -> 50.7 us (0.946)
  Pallas kernels: 52.9 us -> 50 us
    pallas_call x1, Pallas kernels: 52.9 us -> 50 us  [on_device(): pl.pallas_call(kernel, out_shape=pltpu.VMEM((1, SEQ, FEAT), F32), in_spec...]
where the time goes in v3:
time: 50.7 us; the launch traced here: 50.6 us
  Pallas kernels  50 us (99%)
  local copies, waits for them, and re-layouts  0.6 us (1%)
    pallas_call x1, Pallas kernels, on_device(): pl.pallas_call(kernel, out_shape=pltpu.VMEM((1, SEQ, FEAT), F32), in_spec...  50 us

profile of v3, /device:TPU:1, one launch (start us, length us, event | category | flops | bytes accessed | tf_op | source)
XLA Modules:
  0.0 50.6 jit_solution(714982854588049257)
XLA Ops:
  0.0 50.0 %shard_map.109 = f32[1,8,224]{2,1,0:T(8,128)S(1)} custom-call(bf16[1,8,224]{2,1,0:T(8,128)(2,1)} %hidden.1, bf16[1,224,1536]{2,1,0:T(8,128)(2,1)} %query_down.1, bf16[1,224,576]{2,1,0:T(8,128)(2,1)} %latent_down.1, f32[1,1536]{1,0:T(1,128)} %query_gain.1, f32[1,512]{1,0:T(1,128)} %latent_gain.1, bf16[1,1536,1152]{2,1,0:T(8,128)(2,1)} %query_up.1, ...), custom_call_target="tpu_custom_call" | custom-call | flops 400000000 | bytes 11000000 | tf_op jit(solution)/shard_map/pallas_call | solution.py:493
  50.0 0.6 %copy.13 = f32[1,8,224]{2,1,0:T(8,128)} copy(f32[1,8,224]{2,1,0:T(8,128)S(1)} %shard_map.109) | data formatting | bytes 14336

commit v4 on v3

--- a/solution.py
+++ b/solution.py
@@ -30,8 +30,8 @@
 SCALE = (HV + ROPE) ** (-0.5)
 GROUPS = ((0, 1, 7, 2, 6, 3, 5, 4),)
 DIRECT_Q = (1, 7, 2, 6)
-DIRECT_SUM = (2, 6, 1, 7)
-SUM_ORDER = ((4, 3, 5, 0),)
+DIRECT_SUM = (4, 1, 7)
+SUM_ORDER = ((3, 5, 2, 6, 0),)
 ORDER = sum(GROUPS, ())
 STARTS = tuple(sum(len(group) for group in GROUPS[:g]) * NY * 16 for g in range(len(GROUPS)))
 FAR_FIRST = (4, 3, 5, 2, 6, 1, 7, 0)
@@ -139,6 +139,7 @@
     dy_sem,
     ds_sem,
     next_sem,
+    greet_sem,
 ):
     sec = lax.axis_index("section")
     me = lax.axis_index("cache")
@@ -168,38 +169,50 @@
     def wait_bytes(ref, sem):
         pltpu.make_async_copy(ref, ref, sem).wait()
 
+    half = FEAT // 2
+    hid_load = load(hidden.at[0], hid, 0)
+    qd_loads = [
+        load(query_down.at[0, pl.ds(k * half, half)], qd.at[pl.ds(k * half, half)], 1 + 10 * k)
+        for k in range(2)
+    ]
     barrier = pltpu.get_barrier_semaphore()
-    for dz in (4, 3, 5, 2, 6, 1, 7):
+    for dz in (2, NZ - 2, 1, NZ - 1):
         pl.semaphore_signal(barrier, inc=1, device_id=at(dz, 0), device_id_type=MESH)
     for dy in (2, 1, 3):
         pl.semaphore_signal(barrier, inc=1, device_id=at(0, dy), device_id_type=MESH)
     for other in (after, before):
         pl.semaphore_signal(barrier, inc=1, device_id={"section": other}, device_id_type=MESH)
 
-    hid_load = load(hidden.at[0], hid, 0)
-    qd_load = load(query_down.at[0], qd, 1)
     ld_load = load(latent_down.at[0], ld, 2)
     qgain_load = load(query_gain, qgain, 3)
     lgain_load = load(latent_gain, lgain, 4)
     chosen_load = load(selected.at[0], chosen, 5)
     limits_load = load(lengths, limits, 6)
+
+    hid_load.wait()
+    rows = hid[...]
+    for qd_load in qd_loads:
+        qd_load.wait()
     qu_load = load(query_up.at[0], qu, 7)
     kv_load = load(latent_cache.at[0], kv, 8)
     vu_load = load(value_up.at[0], vu, 9)
     op_load = load(output_proj.at[0], op, 10)
-
-    hid_load.wait()
-    rows = hid[...]
-    qd_load.wait()
     wide = jnp.dot(rows, qd[...], preferred_element_type=F32)
     for t in range(QT):
         part_q[t // 3, t % 3] = wide[:, t * 128 : (t + 1) * 128]
 
-    pl.semaphore_wait(barrier, NZ + NY)
+    pl.semaphore_wait(barrier, 4 + NY + 1)
 
     for dy in (2, 1, 3):
         chunk = part_q.at[lax.rem(y + dy, NY)]
         send(chunk, y_q.at[NY - 1 - dy], 0, recv_sem.at[0], at(0, dy))
+    def greet(step):
+        for dz in (2, NZ - 2):
+            pl.semaphore_signal(
+                greet_sem.at[step], inc=1, device_id=at(dz, 0), device_id_type=MESH
+            )
+
+    greet(0)
     ld_load.wait()
     wide = jnp.dot(rows, ld[...], preferred_element_type=F32)
     empty = jnp.zeros((SEQ, 128 - ROPE), F32)
@@ -215,6 +228,7 @@
     x_out[...] = jnp.concatenate([own_rows[:, :128], right_rows], axis=0).astype(BF16)
     send(x_out, x_in, 2, recv_sem.at[2], {"section": after})
 
+    pl.semaphore_wait(greet_sem.at[0], 2)
     wait_bytes(y_q, recv_sem.at[0])
     own_qs[...] = part_q[y] + y_q[0] + y_q[1] + y_q[2]
     for dz in (4, 3, 5, 2, 6, 1, 7):
@@ -535,7 +549,7 @@
             pltpu.VMEM((NC, 16, 128), BF16),
             pltpu.VMEM((16, 128), BF16),
             pltpu.VMEM((16, 128), BF16),
-            dma((11,)),
+            dma((12,)),
             dma((16,)),
             dma((10,)),
             dma((NZ,)),
@@ -544,6 +558,7 @@
             dma((NZ,)),
             dma((len(GROUPS),)),
             pltpu.SemaphoreType.REGULAR,
+            pltpu.SemaphoreType.REGULAR((1,)),
         ],
         compiler_params=pltpu.CompilerParams(
             collective_id=0, has_side_effects=True, vmem_limit_bytes=60 << 20

time: 50.7 us -> 49.9 us (0.984)
  Pallas kernels: 50 us -> 49.2 us
    pallas_call x1, Pallas kernels: 50 us -> 49.2 us  [on_device(): pl.pallas_call(kernel, out_shape=pltpu.VMEM((1, SEQ, FEAT), F32), in_spec...]
where the time goes in v4:
time: 49.9 us; the launch traced here: 49.8 us
  Pallas kernels  49.2 us (99%)
  local copies, waits for them, and re-layouts  0.6 us (1%)
    pallas_call x1, Pallas kernels, on_device(): pl.pallas_call(kernel, out_shape=pltpu.VMEM((1, SEQ, FEAT), F32), in_spec...  49.2 us

profile of v4, /device:TPU:1, one launch (start us, length us, event | category | flops | bytes accessed | tf_op | source)
XLA Modules:
  0.0 49.8 jit_solution(924332509025893045)
XLA Ops:
  0.0 49.2 %shard_map.109 = f32[1,8,224]{2,1,0:T(8,128)S(1)} custom-call(bf16[1,8,224]{2,1,0:T(8,128)(2,1)} %hidden.1, bf16[1,224,1536]{2,1,0:T(8,128)(2,1)} %query_down.1, bf16[1,224,576]{2,1,0:T(8,128)(2,1)} %latent_down.1, f32[1,1536]{1,0:T(1,128)} %query_gain.1, f32[1,512]{1,0:T(1,128)} %latent_gain.1, bf16[1,1536,1152]{2,1,0:T(8,128)(2,1)} %query_up.1, ...), custom_call_target="tpu_custom_call" | custom-call | flops 400000000 | bytes 11000000 | tf_op jit(solution)/shard_map/pallas_call | solution.py:507
  49.2 0.6 %copy.13 = f32[1,8,224]{2,1,0:T(8,128)} copy(f32[1,8,224]{2,1,0:T(8,128)S(1)} %shard_map.109) | data formatting | bytes 14336

commit v5 on v4

--- a/solution.py
+++ b/solution.py
@@ -68,6 +68,24 @@
     top = jnp.where((lane >= 0) & (lane < 3), stats, 0.0)
     total = jnp.where((lane >= 3) & (lane < 6), stats, 0.0)
     return jnp.sum(top, axis=1, keepdims=True), jnp.sum(total, axis=1, keepdims=True)
+
+
+def pack(block, summed, stats, place=0):
+    for t in range(KT):
+        columns = slice(t * 128, (t + 1) * 128)
+        block[t] = summed[:SEQ, columns].astype(BF16)
+        block[KT + t] = summed[SEQ:, columns].astype(BF16)
+    upper = pltpu.roll(stats[:SEQ], 128 - place, axis=1) if place else stats[:SEQ]
+    lower = pltpu.roll(stats[SEQ:], 64 - place, axis=1)
+    block[2 * KT] = (upper + lower).astype(BF16)
+
+
+def unpack(block):
+    tiles = [block[t].astype(F32) for t in range(2 * KT + 1)]
+    upper = jnp.concatenate(tiles[:KT], axis=1)
+    lower = jnp.concatenate(tiles[KT : 2 * KT], axis=1)
+    stats = jnp.concatenate([tiles[-1], pltpu.roll(tiles[-1], 64, axis=1)], axis=0)
+    return jnp.concatenate([upper, lower], axis=0), *read_stats(stats)
 
 
 def merged(parts):
@@ -113,8 +131,6 @@
     lat_q,
     lat_k,
     q_all,
-    q_rope,
-    r_in,
     q_f32,
     o_f32,
     s_f32,
@@ -135,7 +151,6 @@
     recv_sem,
     qz_sem,
     qy_sem,
-    rope_sem,
     dy_sem,
     ds_sem,
     next_sem,
@@ -264,10 +279,12 @@
     first = own[:, :PADKW]
     second = pltpu.roll(own[:, LAT:], PADKW - ROPE, axis=1)
     own_q = jnp.concatenate([first, second], axis=0).astype(BF16)
-    q_all[0] = own_q[:, :LAT]
+    for t in range(KT):
+        q_all[0, t] = first[:, t * 128 : (t + 1) * 128].astype(BF16)
+        q_all[0, KT + t] = second[:, t * 128 : (t + 1) * 128].astype(BF16)
     lane = lax.broadcasted_iota(jnp.int32, (SEQ, 128), 1)
     pair = jnp.where(lane < ROPE, own[:, LAT : LAT + 128], own[:, 2 * KW - 128 :])
-    r_in[0] = jnp.concatenate([pair, jnp.zeros((SEQ, 128), F32)], axis=0).astype(BF16)
+    q_all[0, 2 * KT] = pair.astype(BF16)
 
     for dz in (4, 3, 5, 2, 6, 1, 7):
         r = NZ - dz
@@ -278,9 +295,7 @@
         else:
             send(q_all.at[0], q_all.at[r * NY], 7, qz_sem.at[r], at(dz, 0))
     for dy in (2, 1, 3):
-        send(r_in.at[0], r_in.at[NY - dy], 8, rope_sem.at[0], at(0, dy))
-    for dy in (2, 1, 3):
-        send(q_all.at[0], q_all.at[NY - dy], 9, qy_sem.at[0], at(0, dy))
+        send(q_all.at[0], q_all.at[NY - dy], 8, qy_sem.at[0], at(0, dy))
 
     wait_bytes(lat_k.at[pl.ds(0, NY - 1)], recv_sem.at[6])
     lgain_load.wait()
@@ -313,15 +328,8 @@
         wait_bytes(block, qz_sem.at[r])
         for dy in (2, 1, 3):
             target = q_all.at[r * NY + NY - dy]
-            send(block, target, 9, qy_sem.at[r], at(0, dy))
-
-    wait_bytes(r_in.at[pl.ds(0, NY - 1)], rope_sem.at[0])
-    for k in range(2):
-        two = [r_in[2 * k].astype(F32)[:SEQ], r_in[2 * k + 1].astype(F32)[:SEQ]]
-        q_rope[0, k] = jnp.concatenate(two, axis=0).astype(BF16)
-    for dz in (4, 3, 5, 2, 6, 1, 7):
-        r = NZ - dz
-        send(q_rope.at[0], q_rope.at[r], 10, rope_sem.at[r], at(dz, 0))
+            send(block, target, 8, qy_sem.at[r], at(0, dy))
+
     for r in (1, 7, 2, 6, 3, 5, 4):
         if r not in DIRECT_Q:
             forward(r)
@@ -336,21 +344,16 @@
         for p, r in enumerate(GROUPS[g]):
             arriving = NY if r in DIRECT_Q else NY - 1
             wait_bytes(q_all.at[pl.ds(0, arriving)], qy_sem.at[r])
-            if r > 0:
-                wait_bytes(q_rope.at[r], rope_sem.at[r])
             for k in range(NY):
-                rows_at = base + (p * NY + k) * 16
-                block = q_all[r * NY + k].astype(F32)
+                top_at = base + (p * NY + k) * 16
+                low_at = top_at + SEQ
+                block = q_all.at[r * NY + k]
                 for t in range(KT):
-                    q_f32[t, rows_at : rows_at + 16, :] = block[:, t * 128 : (t + 1) * 128]
-            for k in range(2):
-                two = q_rope[r, k].astype(F32)
-                other = pltpu.roll(two, ROPE, axis=1)
-                for m in range(2):
-                    rows_at = base + (p * NY + 2 * k + m) * 16
-                    own_rows = slice(m * SEQ, (m + 1) * SEQ)
-                    q_f32[KT, rows_at : rows_at + SEQ, :] = two[own_rows]
-                    q_f32[KT, rows_at + SEQ : rows_at + 16, :] = other[own_rows]
+                    q_f32[t, top_at : top_at + SEQ, :] = block[t].astype(F32)
+                    q_f32[t, low_at : low_at + SEQ, :] = block[KT + t].astype(F32)
+                pair = block[2 * KT].astype(F32)
+                q_f32[KT, top_at : top_at + SEQ, :] = pair
+                q_f32[KT, low_at : low_at + SEQ, :] = pltpu.roll(pair, ROPE, axis=1)
         for b in range(SEQ):
             queries = jnp.concatenate(
                 [q_f32[t, pl.ds(base + b, heads, stride=SEQ), :] for t in range(KT + 1)],
@@ -389,23 +392,21 @@
         for k in (2, 1, 3):
             stats = [s_f32[rows_of(g, p, k), :] for p in staged]
             s_out[g, k] = functools.reduce(jnp.add, stats).astype(BF16)
-            send(s_out.at[g, k], ys_in.at[g, NY - 1 - k], 11, ds_sem.at[g], at(0, k))
+            send(s_out.at[g, k], ys_in.at[g, NY - 1 - k], 9, ds_sem.at[g], at(0, k))
         for r in SUM_ORDER[g]:
             p = GROUPS[g].index(r)
             for k in (2, 1, 3):
                 o_out[r, k] = sums_of(g, p, k).astype(BF16)
-                send(o_out.at[r, k], y_in.at[r, NY - 1 - k], 12, dy_sem.at[r], at(0, k))
+                send(o_out.at[r, k], y_in.at[r, NY - 1 - k], 10, dy_sem.at[r], at(0, k))
         for f, r in enumerate(DIRECT_SUM):
             if r in GROUPS[g]:
                 p = GROUPS[g].index(r)
                 to = DIRECT_SUM.index(NZ - r) * NY
                 for k in (2, 1, 3, 0):
                     stats = s_f32[rows_of(g, p, k), :]
-                    stats = pltpu.roll(stats, (128 - 6 * p) % 128, axis=1) if p else stats
-                    wide = jnp.concatenate([sums_of(g, p, k), stats], axis=1)
-                    f_out[f * NY + k] = wide.astype(BF16)
+                    pack(f_out.at[f * NY + k], sums_of(g, p, k), stats, 6 * p)
                     target = f_in.at[to + (NY - k) % NY]
-                    send(f_out.at[f * NY + k], target, 15, recv_sem.at[9], at(r, k))
+                    send(f_out.at[f * NY + k], target, 13, recv_sem.at[9], at(r, k))
 
     def join_sums(g):
         wait_bytes(ys_in.at[g], ds_sem.at[g])
@@ -419,9 +420,8 @@
             summed, top, total = merged(parts)
             if r == 0:
                 return summed, top, total
-            wide = jnp.concatenate([summed, stats_tile(top, total)], axis=1)
-            c_out[r] = wide.astype(BF16)
-            send(c_out.at[r], z_in.at[NZ - r], 13, recv_sem.at[7], at(r, 0))
+            pack(c_out.at[r], summed, stats_tile(top, total))
+            send(c_out.at[r], z_in.at[NZ - r], 11, recv_sem.at[7], at(r, 0))
 
     for g in range(len(GROUPS)):
         attend(g)
@@ -431,17 +431,14 @@
     parts.append((new_key[:, :LAT], new_score, jnp.ones((2 * SEQ, 1), F32)))
 
     def joined_with(parts, blocks):
-        for block in blocks:
-            block = block.astype(F32)
-            parts = parts + [(block[:, :LAT], *read_stats(block[:, LAT:]))]
-        return merged(parts)
+        return merged(parts + [unpack(block) for block in blocks])
 
     if DIRECT_SUM:
         wait_bytes(f_in, recv_sem.at[9])
-        parts = [joined_with(parts, [f_in[k] for k in range(len(DIRECT_SUM) * NY)])]
+        parts = [joined_with(parts, [f_in.at[k] for k in range(len(DIRECT_SUM) * NY)])]
     staged = sum(SUM_ORDER, ())
     wait_bytes(z_in.at[pl.ds(0, len(staged) - 1)], recv_sem.at[7])
-    summed, _, total = joined_with(parts, [z_in[r] for r in range(1, NZ) if r in staged])
+    summed, _, total = joined_with(parts, [z_in.at[r] for r in range(1, NZ) if r in staged])
     attended = summed / total
 
     vu_load.wait()
@@ -468,7 +465,7 @@
             e_out[r * NY + k] = block.astype(BF16)
             slot = (NZ - r) % NZ * NY + y
             target = {"section": after, "cache": zt * NY + k}
-            send(e_out.at[r * NY + k], e_in.at[slot], 14, recv_sem.at[8], target)
+            send(e_out.at[r * NY + k], e_in.at[slot], 12, recv_sem.at[8], target)
 
     wait_bytes(x_in, recv_sem.at[2])
     total = x_in[...].astype(F32)
@@ -487,15 +484,13 @@
     wait_bytes(lat_k.at[pl.ds(0, NY - 1)], send_sem.at[6])
     straight = len(DIRECT_Q)
     wait_bytes(q_all.at[pl.ds(0, NZ - 1 + (NY - 1) * straight)], send_sem.at[7])
-    wait_bytes(r_in.at[pl.ds(0, NY - 1)], send_sem.at[8])
-    wait_bytes(q_all.at[pl.ds(0, (NZ - straight) * (NY - 1))], send_sem.at[9])
-    wait_bytes(q_rope.at[pl.ds(0, NZ - 1)], send_sem.at[10])
-    wait_bytes(ys_in, send_sem.at[11])
-    wait_bytes(y_in.at[pl.ds(0, len(staged))], send_sem.at[12])
-    wait_bytes(z_in.at[pl.ds(0, len(staged) - 1)], send_sem.at[13])
+    wait_bytes(q_all.at[pl.ds(0, (NZ - straight) * (NY - 1))], send_sem.at[8])
+    wait_bytes(ys_in, send_sem.at[9])
+    wait_bytes(y_in.at[pl.ds(0, len(staged))], send_sem.at[10])
+    wait_bytes(z_in.at[pl.ds(0, len(staged) - 1)], send_sem.at[11])
     if DIRECT_SUM:
-        wait_bytes(f_out, send_sem.at[15])
-    wait_bytes(e_out, send_sem.at[14])
+        wait_bytes(f_out, send_sem.at[13])
+    wait_bytes(e_out, send_sem.at[12])
 
 
 def on_device(*arrays):
@@ -531,9 +526,7 @@
             pltpu.VMEM((NZ - 1, 2, SEQ, 128), F32),
             pltpu.VMEM((NY, 3, SEQ, 128), F32),
             pltpu.VMEM((NY, SEQ, 128), F32),
-            pltpu.VMEM((NC, 16, LAT), BF16),
-            pltpu.VMEM((NZ, 2, 16, 128), BF16),
-            pltpu.VMEM((NY, 16, 128), BF16),
+            pltpu.VMEM((NC, 2 * KT + 1, SEQ, 128), BF16),
             pltpu.VMEM((KT + 1, NC * 16, 128), F32),
             pltpu.VMEM((KT, NC * 16, 128), F32),
             pltpu.VMEM((NC * 16, 128), F32),
@@ -541,10 +534,10 @@
             pltpu.VMEM((len(GROUPS), NY, 16, 128), BF16),
             pltpu.VMEM((NZ, NY - 1, 16, LAT), BF16),
             pltpu.VMEM((len(GROUPS), NY - 1, 16, 128), BF16),
-            pltpu.VMEM((NZ, 16, PADKW), BF16),
-            pltpu.VMEM((NZ, 16, PADKW), BF16),
-            pltpu.VMEM((max(1, len(DIRECT_SUM)) * NY, 16, PADKW), BF16),
-            pltpu.VMEM((max(1, len(DIRECT_SUM)) * NY, 16, PADKW), BF16),
+            pltpu.VMEM((NZ, 2 * KT + 1, SEQ, 128), BF16),
+            pltpu.VMEM((NZ, 2 * KT + 1, SEQ, 128), BF16),
+            pltpu.VMEM((max(1, len(DIRECT_SUM)) * NY, 2 * KT + 1, SEQ, 128), BF16),
+            pltpu.VMEM((max(1, len(DIRECT_SUM)) * NY, 2 * KT + 1, SEQ, 128), BF16),
             pltpu.VMEM((NC, 16, 128), BF16),
             pltpu.VMEM((NC, 16, 128), BF16),
             pltpu.VMEM((16, 128), BF16),
@@ -552,7 +545,6 @@
             dma((12,)),
             dma((16,)),
             dma((10,)),
-            dma((NZ,)),
             dma((NZ,)),
             dma((NZ,)),
             dma((NZ,)),

time: 49.9 us -> 49.3 us (0.988)
  Pallas kernels: 49.2 us -> 48.6 us
    pallas_call x1, Pallas kernels: 49.2 us -> 48.6 us  [on_device(): pl.pallas_call(kernel, out_shape=pltpu.VMEM((1, SEQ, FEAT), F32), in_spec...]
where the time goes in v5:
time: 49.3 us; the launch traced here: 49.2 us
  Pallas kernels  48.6 us (99%)
  local copies, waits for them, and re-layouts  0.6 us (1%)
    pallas_call x1, Pallas kernels, on_device(): pl.pallas_call(kernel, out_shape=pltpu.VMEM((1, SEQ, FEAT), F32), in_spec...  48.6 us

profile of v5, /device:TPU:1, one launch (start us, length us, event | category | flops | bytes accessed | tf_op | source)
XLA Modules:
  0.0 49.2 jit_solution(11785977521667876198)
XLA Ops:
  0.0 48.6 %shard_map.109 = f32[1,8,224]{2,1,0:T(8,128)S(1)} custom-call(bf16[1,8,224]{2,1,0:T(8,128)(2,1)} %hidden.1, bf16[1,224,1536]{2,1,0:T(8,128)(2,1)} %query_down.1, bf16[1,224,576]{2,1,0:T(8,128)(2,1)} %latent_down.1, f32[1,1536]{1,0:T(1,128)} %query_gain.1, f32[1,512]{1,0:T(1,128)} %latent_gain.1, bf16[1,1536,1152]{2,1,0:T(8,128)(2,1)} %query_up.1, ...), custom_call_target="tpu_custom_call" | custom-call | flops 400000000 | bytes 11000000 | tf_op jit(solution)/shard_map/pallas_call | solution.py:502
  48.6 0.6 %copy.13 = f32[1,8,224]{2,1,0:T(8,128)} copy(f32[1,8,224]{2,1,0:T(8,128)S(1)} %shard_map.109) | data formatting | bytes 14336
